TPU v7x, 512 devices: a whole 4x8x8 slice. The times are simulated.
512 devices in a mesh: tm: 64 (over z, x, y_hi), head: 8 (over y_lo, core).
Axes of the slice: x: 4, y: 8 (y_hi: 2, y_lo: 4; y = y_hi * 4 + y_lo), z: 8, core: 2. Of those that a mesh axis runs over, the one named last changes fastest.
Arguments:
- queries: bfloat16 [8192, 8192], P(('tm', 'head')), may hold values from -160 to 160
- vis_keys: bfloat16 [16384, 1024], P('tm', 'head'), may hold values from -15 to 15
- vis_values: bfloat16 [16384, 1024], P('tm', 'head'), may hold values from -6 to 6
- span_start: int32 [8192], P('tm'), may hold values from 0 to 63, as said below
- span_end: int32 [8192], P('tm'), may hold values from 0 to 63, as said below
Outputs:
- context: bfloat16 [8192, 8192], P(('tm', 'head'))
Inputs may be any that keep to these rules, and one draw needn't show every extreme that they name: Row r's span [span_start[r], span_end[r]] holds 1 to 6 shards and contains the row's own shard r // 128; some row reaches 6 shards. span_end[r] >= span_start[r], as described for span_start.
All inputs are finite; a program needn't handle non-finite values.
Results may differ from a plain program's by a relative error of at most 0.004.
Values may be sent and summed in bfloat16 or wider, within the bound.
A program may use at most 64 MiB of HBM per device.

v0:
```python
import math

import jax
import jax.numpy as jnp
from jax import lax
from jax.sharding import PartitionSpec as P

HEADS = 64
KV_HEADS = 8
HEAD_DIM = 128
SPAN = 6


def shifted(block, axis, distance):
    devices = range(lax.axis_size(axis))
    route = [(i - distance, i) for i in devices if i - distance in devices]
    return lax.ppermute(block, axis, route)


def shards(queries, vis_keys, vis_values, span_start, span_end):
    by_head = lax.all_to_all(queries, "head", split_axis=1, concat_axis=0, tiled=True)
    row_count = by_head.shape[0]
    local_kv = vis_keys.shape[1] // HEAD_DIM
    group_size = HEADS // KV_HEADS
    grouped = by_head.reshape(row_count, local_kv, group_size, HEAD_DIM)
    position = lax.axis_index("tm")
    root_dim = math.sqrt(HEAD_DIM)

    def absorb(state, key_block, value_block, shard_index):
        running_max, running_sum, accumulated = state
        key_heads = key_block.reshape(-1, local_kv, HEAD_DIM)
        value_heads = value_block.reshape(-1, local_kv, HEAD_DIM)
        scores = (
            jnp.einsum("rjgd,kjd->rjgk", grouped, key_heads, preferred_element_type=jnp.float32)
            / root_dim
        )
        in_span = (span_start <= shard_index) & (shard_index <= span_end)
        block_max = jnp.where(in_span[:, None, None], jnp.max(scores, axis=-1), -1e30)
        updated_max = jnp.maximum(running_max, block_max)
        weights = jnp.where(
            in_span[:, None, None, None], jnp.exp(scores - updated_max[..., None]), 0.0
        )
        rescale = jnp.exp(running_max - updated_max)
        running_sum = running_sum * rescale + jnp.sum(weights, axis=-1)
        rounded = weights.astype(jnp.bfloat16)
        product = jnp.einsum(
            "rjgk,kjd->rjgd", rounded, value_heads, preferred_element_type=jnp.float32
        )
        accumulated = accumulated * rescale[..., None] + product
        return (updated_max, running_sum, accumulated)

    def visit_block(state, key_block, value_block, shard_index):
        return absorb(state, key_block, value_block, shard_index)

    start_state = (
        jnp.full((row_count, local_kv, group_size), -1e30, jnp.float32),
        jnp.zeros((row_count, local_kv, group_size), jnp.float32),
        jnp.zeros((row_count, local_kv, group_size, HEAD_DIM), jnp.float32),
    )
    state = visit_block(start_state, vis_keys, vis_values, position)
    for distance in range(1, SPAN):
        for direction in (1, -1):
            fetched = shifted((vis_keys, vis_values), "tm", -direction * distance)
            state = visit_block(state, fetched[0], fetched[1], position + direction * distance)
    context = state[2] / state[1][..., None]
    context = context.reshape(row_count, local_kv * group_size * HEAD_DIM).astype(jnp.bfloat16)
    return lax.all_to_all(context, "head", split_axis=0, concat_axis=1, tiled=True)


def solution(mesh):
    return jax.shard_map(
        shards,
        mesh=mesh,
        in_specs=(P(("tm", "head"), None), P("tm", "head"), P("tm", "head"), P("tm"), P("tm")),
        out_specs=P(("tm", "head"), None),
        check_vma=False,
    )
```

profile of v0, /device:TPU:255, one launch (start us, length us, event | category | flops | bytes accessed | tf_op | source)
XLA Modules:
  0.0 152.7 jit_solution(16973207675491376358)
XLA Ops:
  0.0 1.7 %copy.125 = bf16[2,8,8,1024]{3,2,0,1:T(8,128)(2,1)} copy(bf16[2,8,8,1024]{3,2,1,0:T(8,128)(2,1)} %bitcast.307) | data formatting | bytes 524288 | tf_op jit(solution)/shard_map/all_to_all | solution.py:21
  1.7 6.7 %all-to-all-start = ((bf16[16,8,1024]{2,0,1:T(8,128)(2,1)}), bf16[16,8,1024]{2,0,1:T(8,128)(2,1)S(1)}, u32[]{:S(2)}, u32[]{:S(2)}) async-start(bf16[16,8,1024]{2,0,1:T(8,128)(2,1)} %bitcast.293), calls=%async_computation | async-start | bytes 524288 | tf_op jit(solution)/shard_map/all_to_all | solution.py:21
  8.4 6.5 %collective-permute-start.18 = (bf16[256,128]{1,0:T(8,128)(2,1)S(1)}, bf16[256,128]{1,0:T(8,128)(2,1)S(1)}, u32[]{:S(2)}, u32[]{:S(2)}) collective-permute-start(bf16[256,128]{1,0:T(8,128)(2,1)S(1)} %copy-done.1), channel_id=1, source_target_pairs={{0,40},{8,48},{16,56},{24,64},{32,72},{40,80},{48,88},{56,96},{64,... | collective-permute-start | bytes 196616 | tf_op jit(solution)/shard_map/ppermute | solution.py:17
  14.9 5.0 %collective-permute-start.16 = (bf16[256,128]{1,0:T(8,128)(2,1)S(1)}, bf16[256,128]{1,0:T(8,128)(2,1)S(1)}, u32[]{:S(2)}, u32[]{:S(2)}) collective-permute-start(bf16[256,128]{1,0:T(8,128)(2,1)S(1)} %copy-done.1), channel_id=1, source_target_pairs={{40,0},{48,8},{56,16},{64,24},{72,32},{80,40},{88,48},{96,56},{104... | collective-permute-start | bytes 196616 | tf_op jit(solution)/shard_map/ppermute | solution.py:17
  20.0 8.2 %collective-permute-start.14 = (bf16[256,128]{1,0:T(8,128)(2,1)S(1)}, bf16[256,128]{1,0:T(8,128)(2,1)S(1)}, u32[]{:S(2)}, u32[]{:S(2)}) collective-permute-start(bf16[256,128]{1,0:T(8,128)(2,1)S(1)} %copy-done.1), channel_id=1, source_target_pairs={{0,32},{8,40},{16,48},{24,56},{32,64},{40,72},{48,80},{56,88},{64,... | collective-permute-start | bytes 196616 | tf_op jit(solution)/shard_map/ppermute | solution.py:17
  28.2 1.9 %collective-permute-start.12 = (bf16[256,128]{1,0:T(8,128)(2,1)S(1)}, bf16[256,128]{1,0:T(8,128)(2,1)S(1)}, u32[]{:S(2)}, u32[]{:S(2)}) collective-permute-start(bf16[256,128]{1,0:T(8,128)(2,1)S(1)} %copy-done.1), channel_id=1, source_target_pairs={{32,0},{40,8},{48,16},{56,24},{64,32},{72,40},{80,48},{88,56},{96,... | collective-permute-start | bytes 196616 | tf_op jit(solution)/shard_map/ppermute | solution.py:17
  30.1 6.5 %collective-permute-start.10 = (bf16[256,128]{1,0:T(8,128)(2,1)S(1)}, bf16[256,128]{1,0:T(8,128)(2,1)S(1)}, u32[]{:S(2)}, u32[]{:S(2)}) collective-permute-start(bf16[256,128]{1,0:T(8,128)(2,1)S(1)} %copy-done.1), channel_id=1, source_target_pairs={{0,24},{8,32},{16,40},{24,48},{32,56},{40,64},{48,72},{56,80},{64,... | collective-permute-start | bytes 196616 | tf_op jit(solution)/shard_map/ppermute | solution.py:17
  36.7 0.6 copy-done.2
  37.4 0.3 fusion.165
  37.7 3.5 %collective-permute-start.8 = (bf16[256,128]{1,0:T(8,128)(2,1)S(1)}, bf16[256,128]{1,0:T(8,128)(2,1)S(1)}, u32[]{:S(2)}, u32[]{:S(2)}) collective-permute-start(bf16[256,128]{1,0:T(8,128)(2,1)S(1)} %copy-done.1), channel_id=1, source_target_pairs={{24,0},{32,8},{40,16},{48,24},{56,32},{64,40},{72,48},{80,56},{88,... | collective-permute-start | bytes 196616 | tf_op jit(solution)/shard_map/ppermute | solution.py:17
  41.6 9.4 %collective-permute-start.6 = (bf16[256,128]{1,0:T(8,128)(2,1)S(1)}, bf16[256,128]{1,0:T(8,128)(2,1)S(1)}, u32[]{:S(2)}, u32[]{:S(2)}) collective-permute-start(bf16[256,128]{1,0:T(8,128)(2,1)S(1)} %copy-done.1), channel_id=1, source_target_pairs={{0,16},{8,24},{16,32},{24,40},{32,48},{40,56},{48,64},{56,72},{64,... | collective-permute-start | bytes 196616 | tf_op jit(solution)/shard_map/ppermute | solution.py:17
  51.0 0.3 fusion.157
  51.3 1.9 %collective-permute-start.4 = (bf16[256,128]{1,0:T(8,128)(2,1)S(1)}, bf16[256,128]{1,0:T(8,128)(2,1)S(1)}, u32[]{:S(2)}, u32[]{:S(2)}) collective-permute-start(bf16[256,128]{1,0:T(8,128)(2,1)S(1)} %copy-done.1), channel_id=1, source_target_pairs={{16,0},{24,8},{32,16},{40,24},{48,32},{56,40},{64,48},{72,56},{80,... | collective-permute-start | bytes 196616 | tf_op jit(solution)/shard_map/ppermute | solution.py:17
  53.6 6.6 %collective-permute-start.2 = (bf16[256,128]{1,0:T(8,128)(2,1)S(1)}, bf16[256,128]{1,0:T(8,128)(2,1)S(1)}, u32[]{:S(2)}, u32[]{:S(2)}) collective-permute-start(bf16[256,128]{1,0:T(8,128)(2,1)S(1)} %copy-done.1), channel_id=1, source_target_pairs={{0,8},{8,16},{16,24},{24,32},{32,40},{40,48},{48,56},{56,64},{64,7... | collective-permute-start | bytes 196616 | tf_op jit(solution)/shard_map/ppermute | solution.py:17
  60.5 2.6 %collective-permute-start = (bf16[256,128]{1,0:T(8,128)(2,1)S(1)}, bf16[256,128]{1,0:T(8,128)(2,1)S(1)}, u32[]{:S(2)}, u32[]{:S(2)}) collective-permute-start(bf16[256,128]{1,0:T(8,128)(2,1)S(1)} %copy-done.1), channel_id=1, source_target_pairs={{8,0},{16,8},{24,16},{32,24},{40,32},{48,40},{56,48},{64,56},{72,6... | collective-permute-start | bytes 196616 | tf_op jit(solution)/shard_map/ppermute | solution.py:17
  63.4 1.9 %collective-permute-start.13 = (bf16[256,128]{1,0:T(8,128)(2,1)S(1)}, bf16[256,128]{1,0:T(8,128)(2,1)S(1)}, u32[]{:S(2)}, u32[]{:S(2)}) collective-permute-start(bf16[256,128]{1,0:T(8,128)(2,1)S(1)} %copy-done), channel_id=1, source_target_pairs={{32,0},{40,8},{48,16},{56,24},{64,32},{72,40},{80,48},{88,56},{96,... | collective-permute-start | bytes 196616 | tf_op jit(solution)/shard_map/ppermute | solution.py:17
  65.4 0.3 fusion.161
  65.7 7.7 %collective-permute-start.11 = (bf16[256,128]{1,0:T(8,128)(2,1)S(1)}, bf16[256,128]{1,0:T(8,128)(2,1)S(1)}, u32[]{:S(2)}, u32[]{:S(2)}) collective-permute-start(bf16[256,128]{1,0:T(8,128)(2,1)S(1)} %copy-done), channel_id=1, source_target_pairs={{0,24},{8,32},{16,40},{24,48},{32,56},{40,64},{48,72},{56,80},{64,... | collective-permute-start | bytes 196616 | tf_op jit(solution)/shard_map/ppermute | solution.py:17
  73.4 0.3 fusion.162
  73.8 2.4 %collective-permute-start.9 = (bf16[256,128]{1,0:T(8,128)(2,1)S(1)}, bf16[256,128]{1,0:T(8,128)(2,1)S(1)}, u32[]{:S(2)}, u32[]{:S(2)}) collective-permute-start(bf16[256,128]{1,0:T(8,128)(2,1)S(1)} %copy-done), channel_id=1, source_target_pairs={{24,0},{32,8},{40,16},{48,24},{56,32},{64,40},{72,48},{80,56},{88,... | collective-permute-start | bytes 196616 | tf_op jit(solution)/shard_map/ppermute | solution.py:17
  76.1 0.3 fusion.163
  76.5 10.0 %collective-permute-start.7 = (bf16[256,128]{1,0:T(8,128)(2,1)S(1)}, bf16[256,128]{1,0:T(8,128)(2,1)S(1)}, u32[]{:S(2)}, u32[]{:S(2)}) collective-permute-start(bf16[256,128]{1,0:T(8,128)(2,1)S(1)} %copy-done), channel_id=1, source_target_pairs={{0,16},{8,24},{16,32},{24,40},{32,48},{40,56},{48,64},{56,72},{64,... | collective-permute-start | bytes 196616 | tf_op jit(solution)/shard_map/ppermute | solution.py:17
  86.5 0.3 fusion.164
  86.8 1.9 %collective-permute-start.5 = (bf16[256,128]{1,0:T(8,128)(2,1)S(1)}, bf16[256,128]{1,0:T(8,128)(2,1)S(1)}, u32[]{:S(2)}, u32[]{:S(2)}) collective-permute-start(bf16[256,128]{1,0:T(8,128)(2,1)S(1)} %copy-done), channel_id=1, source_target_pairs={{16,0},{24,8},{32,16},{40,24},{48,32},{56,40},{64,48},{72,56},{80,... | collective-permute-start | bytes 196616 | tf_op jit(solution)/shard_map/ppermute | solution.py:17
  89.3 0.4 fusion.35
  89.6 0.4 fusion.39
  90.0 0.4 fusion.43
  90.4 0.4 fusion.47
  90.8 0.4 fusion.51
  91.2 0.6 fusion.12
  91.9 11.1 %collective-permute-start.3 = (bf16[256,128]{1,0:T(8,128)(2,1)S(1)}, bf16[256,128]{1,0:T(8,128)(2,1)S(1)}, u32[]{:S(2)}, u32[]{:S(2)}) collective-permute-start(bf16[256,128]{1,0:T(8,128)(2,1)S(1)} %copy-done), channel_id=1, source_target_pairs={{0,8},{8,16},{16,24},{24,32},{32,40},{40,48},{48,56},{56,64},{64,7... | collective-permute-start | bytes 196616 | tf_op jit(solution)/shard_map/ppermute | solution.py:17
  102.9 0.4 convolution_bitcast_fusion.3
  103.3 1.9 %collective-permute-start.15 = (bf16[256,128]{1,0:T(8,128)(2,1)S(1)}, bf16[256,128]{1,0:T(8,128)(2,1)S(1)}, u32[]{:S(2)}, u32[]{:S(2)}) collective-permute-start(bf16[256,128]{1,0:T(8,128)(2,1)S(1)} %copy-done), channel_id=1, source_target_pairs={{0,32},{8,40},{16,48},{24,56},{32,64},{40,72},{48,80},{56,88},{64,... | collective-permute-start | bytes 196616 | tf_op jit(solution)/shard_map/ppermute | solution.py:17
  105.3 0.4 convolution_bitcast_fusion.4
  105.6 1.9 %collective-permute-start.17 = (bf16[256,128]{1,0:T(8,128)(2,1)S(1)}, bf16[256,128]{1,0:T(8,128)(2,1)S(1)}, u32[]{:S(2)}, u32[]{:S(2)}) collective-permute-start(bf16[256,128]{1,0:T(8,128)(2,1)S(1)} %copy-done), channel_id=1, source_target_pairs={{40,0},{48,8},{56,16},{64,24},{72,32},{80,40},{88,48},{96,56},{104... | collective-permute-start | bytes 196616 | tf_op jit(solution)/shard_map/ppermute | solution.py:17
  107.6 0.4 convolution_bitcast_fusion.5
  108.0 10.3 %collective-permute-start.19 = (bf16[256,128]{1,0:T(8,128)(2,1)S(1)}, bf16[256,128]{1,0:T(8,128)(2,1)S(1)}, u32[]{:S(2)}, u32[]{:S(2)}) collective-permute-start(bf16[256,128]{1,0:T(8,128)(2,1)S(1)} %copy-done), channel_id=1, source_target_pairs={{0,40},{8,48},{16,56},{24,64},{32,72},{40,80},{48,88},{56,96},{64,... | collective-permute-start | bytes 196616 | tf_op jit(solution)/shard_map/ppermute | solution.py:17
  118.2 0.4 convolution_bitcast_fusion.6
  118.6 1.9 %collective-permute-start.1 = (bf16[256,128]{1,0:T(8,128)(2,1)S(1)}, bf16[256,128]{1,0:T(8,128)(2,1)S(1)}, u32[]{:S(2)}, u32[]{:S(2)}) collective-permute-start(bf16[256,128]{1,0:T(8,128)(2,1)S(1)} %copy-done), channel_id=1, source_target_pairs={{8,0},{16,8},{24,16},{32,24},{40,32},{48,40},{56,48},{64,56},{72,6... | collective-permute-start | bytes 196616 | tf_op jit(solution)/shard_map/ppermute | solution.py:17
  120.6 0.4 convolution_bitcast_fusion.7
  120.9 0.4 convolution_bitcast_fusion.8
  121.3 0.4 convolution_bitcast_fusion.2
  121.7 0.4 convolution_bitcast_fusion.1
  122.1 0.4 convolution_bitcast_fusion
  122.5 9.3 %collective-permute-done.1 = bf16[256,128]{1,0:T(8,128)(2,1)S(1)} collective-permute-done((bf16[256,128]{1,0:T(8,128)(2,1)S(1)}, bf16[256,128]{1,0:T(8,128)(2,1)S(1)}, u32[]{:S(2)}, u32[]{:S(2)}) %collective-permute-start.1) | collective-permute-done | bytes 65568 | tf_op jit(solution)/shard_map/ppermute | solution.py:17
  131.8 2.0 %fusion.34 = bf16[128,1,8,128]{3,0,2,1:T(8,128)(2,1)S(1)} fusion(f32[128,1,8,128]{3,0,2,1:T(8,128)S(1)} %convolution_bitcast_fusion, f32[128,1,8,128]{3,0,2,1:T(8,128)S(1)} %convolution_bitcast_fusion.1, f32[128,1,8,128]{3,0,2,1:T(8,128)S(1)} %convolution_bitcast_fusion.2, f32[1,128,128,8]{1,2,3,0:T(8,128)S(1)} %convolution_bitcast_fusion.3, ...), kind=kOutput, calls=%fused_computation.56 | convolution fusion | flops 70647808 | bytes 6664320 | tf_op jit(solution)/shard_map/rjgk,kjd->rjgd/dot_general | solution.py:46
  134.1 17.9 %all_to_all.32 = bf16[8,16,1024]{2,1,0:T(8,128)(2,1)S(1)} all-to-all(bf16[8,16,1024]{2,1,0:T(8,128)(2,1)S(1)} %convert_element_type.52), channel_id=1, replica_groups=mesh['tm'=64,'head'=8] {'head'}, dimensions={0} | all-to-all | bytes 524288 | tf_op jit(solution)/shard_map/all_to_all | solution.py:67
  152.0 0.7 copy.78
  (40 shorter events, 2.2 us)
Async XLA Ops:
  1.7 6.7 %copy-start.1 = (bf16[256,128]{1,0:T(8,128)(2,1)S(1)}, bf16[256,128]{1,0:T(8,128)(2,1)}, u32[]{:S(2)}) copy-start(bf16[256,128]{1,0:T(8,128)(2,1)} %param.6) | copy-start | bytes 196612
  1.7 35.7 %all-to-all-start = ((bf16[16,8,1024]{2,0,1:T(8,128)(2,1)}), bf16[16,8,1024]{2,0,1:T(8,128)(2,1)S(1)}, u32[]{:S(2)}, u32[]{:S(2)}) async-start(bf16[16,8,1024]{2,0,1:T(8,128)(2,1)} %bitcast.293), calls=%async_computation | async-start | bytes 524288 | tf_op jit(solution)/shard_map/all_to_all | solution.py:21
  8.4 29.3 %collective-permute-start.18 = (bf16[256,128]{1,0:T(8,128)(2,1)S(1)}, bf16[256,128]{1,0:T(8,128)(2,1)S(1)}, u32[]{:S(2)}, u32[]{:S(2)}) collective-permute-start(bf16[256,128]{1,0:T(8,128)(2,1)S(1)} %copy-done.1), channel_id=1, source_target_pairs={{0,40},{8,48},{16,56},{24,64},{32,72},{40,80},{48,88},{56,96},{64,... | collective-permute-start | bytes 196616 | tf_op jit(solution)/shard_map/ppermute | solution.py:17
  14.9 26.7 %collective-permute-start.16 = (bf16[256,128]{1,0:T(8,128)(2,1)S(1)}, bf16[256,128]{1,0:T(8,128)(2,1)S(1)}, u32[]{:S(2)}, u32[]{:S(2)}) collective-permute-start(bf16[256,128]{1,0:T(8,128)(2,1)S(1)} %copy-done.1), channel_id=1, source_target_pairs={{40,0},{48,8},{56,16},{64,24},{72,32},{80,40},{88,48},{96,56},{104... | collective-permute-start | bytes 196616 | tf_op jit(solution)/shard_map/ppermute | solution.py:17
  20.0 31.3 %collective-permute-start.14 = (bf16[256,128]{1,0:T(8,128)(2,1)S(1)}, bf16[256,128]{1,0:T(8,128)(2,1)S(1)}, u32[]{:S(2)}, u32[]{:S(2)}) collective-permute-start(bf16[256,128]{1,0:T(8,128)(2,1)S(1)} %copy-done.1), channel_id=1, source_target_pairs={{0,32},{8,40},{16,48},{24,56},{32,64},{40,72},{48,80},{56,88},{64,... | collective-permute-start | bytes 196616 | tf_op jit(solution)/shard_map/ppermute | solution.py:17
  28.2 25.4 %collective-permute-start.12 = (bf16[256,128]{1,0:T(8,128)(2,1)S(1)}, bf16[256,128]{1,0:T(8,128)(2,1)S(1)}, u32[]{:S(2)}, u32[]{:S(2)}) collective-permute-start(bf16[256,128]{1,0:T(8,128)(2,1)S(1)} %copy-done.1), channel_id=1, source_target_pairs={{32,0},{40,8},{48,16},{56,24},{64,32},{72,40},{80,48},{88,56},{96,... | collective-permute-start | bytes 196616 | tf_op jit(solution)/shard_map/ppermute | solution.py:17
  30.1 30.4 %collective-permute-start.10 = (bf16[256,128]{1,0:T(8,128)(2,1)S(1)}, bf16[256,128]{1,0:T(8,128)(2,1)S(1)}, u32[]{:S(2)}, u32[]{:S(2)}) collective-permute-start(bf16[256,128]{1,0:T(8,128)(2,1)S(1)} %copy-done.1), channel_id=1, source_target_pairs={{0,24},{8,32},{16,40},{24,48},{32,56},{40,64},{48,72},{56,80},{64,... | collective-permute-start | bytes 196616 | tf_op jit(solution)/shard_map/ppermute | solution.py:17
  36.6 0.7 copy-start.2
  36.7 0.7 copy-start.3
  37.7 25.7 %collective-permute-start.8 = (bf16[256,128]{1,0:T(8,128)(2,1)S(1)}, bf16[256,128]{1,0:T(8,128)(2,1)S(1)}, u32[]{:S(2)}, u32[]{:S(2)}) collective-permute-start(bf16[256,128]{1,0:T(8,128)(2,1)S(1)} %copy-done.1), channel_id=1, source_target_pairs={{24,0},{32,8},{40,16},{48,24},{56,32},{64,40},{72,48},{80,56},{88,... | collective-permute-start | bytes 196616 | tf_op jit(solution)/shard_map/ppermute | solution.py:17
  41.6 24.1 %collective-permute-start.6 = (bf16[256,128]{1,0:T(8,128)(2,1)S(1)}, bf16[256,128]{1,0:T(8,128)(2,1)S(1)}, u32[]{:S(2)}, u32[]{:S(2)}) collective-permute-start(bf16[256,128]{1,0:T(8,128)(2,1)S(1)} %copy-done.1), channel_id=1, source_target_pairs={{0,16},{8,24},{16,32},{24,40},{32,48},{40,56},{48,64},{56,72},{64,... | collective-permute-start | bytes 196616 | tf_op jit(solution)/shard_map/ppermute | solution.py:17
  51.3 22.4 %collective-permute-start.4 = (bf16[256,128]{1,0:T(8,128)(2,1)S(1)}, bf16[256,128]{1,0:T(8,128)(2,1)S(1)}, u32[]{:S(2)}, u32[]{:S(2)}) collective-permute-start(bf16[256,128]{1,0:T(8,128)(2,1)S(1)} %copy-done.1), channel_id=1, source_target_pairs={{16,0},{24,8},{32,16},{40,24},{48,32},{56,40},{64,48},{72,56},{80,... | collective-permute-start | bytes 196616 | tf_op jit(solution)/shard_map/ppermute | solution.py:17
  53.6 22.9 %collective-permute-start.2 = (bf16[256,128]{1,0:T(8,128)(2,1)S(1)}, bf16[256,128]{1,0:T(8,128)(2,1)S(1)}, u32[]{:S(2)}, u32[]{:S(2)}) collective-permute-start(bf16[256,128]{1,0:T(8,128)(2,1)S(1)} %copy-done.1), channel_id=1, source_target_pairs={{0,8},{8,16},{16,24},{24,32},{32,40},{40,48},{48,56},{56,64},{64,7... | collective-permute-start | bytes 196616 | tf_op jit(solution)/shard_map/ppermute | solution.py:17
  60.4 3.0 %copy-start = (bf16[256,128]{1,0:T(8,128)(2,1)S(1)}, bf16[256,128]{1,0:T(8,128)(2,1)}, u32[]{:S(2)}) copy-start(bf16[256,128]{1,0:T(8,128)(2,1)} %param.7) | copy-start | bytes 196612
  60.5 26.3 %collective-permute-start = (bf16[256,128]{1,0:T(8,128)(2,1)S(1)}, bf16[256,128]{1,0:T(8,128)(2,1)S(1)}, u32[]{:S(2)}, u32[]{:S(2)}) collective-permute-start(bf16[256,128]{1,0:T(8,128)(2,1)S(1)} %copy-done.1), channel_id=1, source_target_pairs={{8,0},{16,8},{24,16},{32,24},{40,32},{48,40},{56,48},{64,56},{72,6... | collective-permute-start | bytes 196616 | tf_op jit(solution)/shard_map/ppermute | solution.py:17
  63.4 28.4 %collective-permute-start.13 = (bf16[256,128]{1,0:T(8,128)(2,1)S(1)}, bf16[256,128]{1,0:T(8,128)(2,1)S(1)}, u32[]{:S(2)}, u32[]{:S(2)}) collective-permute-start(bf16[256,128]{1,0:T(8,128)(2,1)S(1)} %copy-done), channel_id=1, source_target_pairs={{32,0},{40,8},{48,16},{56,24},{64,32},{72,40},{80,48},{88,56},{96,... | collective-permute-start | bytes 196616 | tf_op jit(solution)/shard_map/ppermute | solution.py:17
  65.7 37.6 %collective-permute-start.11 = (bf16[256,128]{1,0:T(8,128)(2,1)S(1)}, bf16[256,128]{1,0:T(8,128)(2,1)S(1)}, u32[]{:S(2)}, u32[]{:S(2)}) collective-permute-start(bf16[256,128]{1,0:T(8,128)(2,1)S(1)} %copy-done), channel_id=1, source_target_pairs={{0,24},{8,32},{16,40},{24,48},{32,56},{40,64},{48,72},{56,80},{64,... | collective-permute-start | bytes 196616 | tf_op jit(solution)/shard_map/ppermute | solution.py:17
  73.8 31.9 %collective-permute-start.9 = (bf16[256,128]{1,0:T(8,128)(2,1)S(1)}, bf16[256,128]{1,0:T(8,128)(2,1)S(1)}, u32[]{:S(2)}, u32[]{:S(2)}) collective-permute-start(bf16[256,128]{1,0:T(8,128)(2,1)S(1)} %copy-done), channel_id=1, source_target_pairs={{24,0},{32,8},{40,16},{48,24},{56,32},{64,40},{72,48},{80,56},{88,... | collective-permute-start | bytes 196616 | tf_op jit(solution)/shard_map/ppermute | solution.py:17
  76.5 31.5 %collective-permute-start.7 = (bf16[256,128]{1,0:T(8,128)(2,1)S(1)}, bf16[256,128]{1,0:T(8,128)(2,1)S(1)}, u32[]{:S(2)}, u32[]{:S(2)}) collective-permute-start(bf16[256,128]{1,0:T(8,128)(2,1)S(1)} %copy-done), channel_id=1, source_target_pairs={{0,16},{8,24},{16,32},{24,40},{32,48},{40,56},{48,64},{56,72},{64,... | collective-permute-start | bytes 196616 | tf_op jit(solution)/shard_map/ppermute | solution.py:17
  86.8 31.8 %collective-permute-start.5 = (bf16[256,128]{1,0:T(8,128)(2,1)S(1)}, bf16[256,128]{1,0:T(8,128)(2,1)S(1)}, u32[]{:S(2)}, u32[]{:S(2)}) collective-permute-start(bf16[256,128]{1,0:T(8,128)(2,1)S(1)} %copy-done), channel_id=1, source_target_pairs={{16,0},{24,8},{32,16},{40,24},{48,32},{56,40},{64,48},{72,56},{80,... | collective-permute-start | bytes 196616 | tf_op jit(solution)/shard_map/ppermute | solution.py:17
  91.9 29.1 %collective-permute-start.3 = (bf16[256,128]{1,0:T(8,128)(2,1)S(1)}, bf16[256,128]{1,0:T(8,128)(2,1)S(1)}, u32[]{:S(2)}, u32[]{:S(2)}) collective-permute-start(bf16[256,128]{1,0:T(8,128)(2,1)S(1)} %copy-done), channel_id=1, source_target_pairs={{0,8},{8,16},{16,24},{24,32},{32,40},{40,48},{48,56},{56,64},{64,7... | collective-permute-start | bytes 196616 | tf_op jit(solution)/shard_map/ppermute | solution.py:17
  103.3 18.0 %collective-permute-start.15 = (bf16[256,128]{1,0:T(8,128)(2,1)S(1)}, bf16[256,128]{1,0:T(8,128)(2,1)S(1)}, u32[]{:S(2)}, u32[]{:S(2)}) collective-permute-start(bf16[256,128]{1,0:T(8,128)(2,1)S(1)} %copy-done), channel_id=1, source_target_pairs={{0,32},{8,40},{16,48},{24,56},{32,64},{40,72},{48,80},{56,88},{64,... | collective-permute-start | bytes 196616 | tf_op jit(solution)/shard_map/ppermute | solution.py:17
  105.6 16.1 %collective-permute-start.17 = (bf16[256,128]{1,0:T(8,128)(2,1)S(1)}, bf16[256,128]{1,0:T(8,128)(2,1)S(1)}, u32[]{:S(2)}, u32[]{:S(2)}) collective-permute-start(bf16[256,128]{1,0:T(8,128)(2,1)S(1)} %copy-done), channel_id=1, source_target_pairs={{40,0},{48,8},{56,16},{64,24},{72,32},{80,40},{88,48},{96,56},{104... | collective-permute-start | bytes 196616 | tf_op jit(solution)/shard_map/ppermute | solution.py:17
  108.0 14.1 %collective-permute-start.19 = (bf16[256,128]{1,0:T(8,128)(2,1)S(1)}, bf16[256,128]{1,0:T(8,128)(2,1)S(1)}, u32[]{:S(2)}, u32[]{:S(2)}) collective-permute-start(bf16[256,128]{1,0:T(8,128)(2,1)S(1)} %copy-done), channel_id=1, source_target_pairs={{0,40},{8,48},{16,56},{24,64},{32,72},{40,80},{48,88},{56,96},{64,... | collective-permute-start | bytes 196616 | tf_op jit(solution)/shard_map/ppermute | solution.py:17
  118.6 13.1 %collective-permute-start.1 = (bf16[256,128]{1,0:T(8,128)(2,1)S(1)}, bf16[256,128]{1,0:T(8,128)(2,1)S(1)}, u32[]{:S(2)}, u32[]{:S(2)}) collective-permute-start(bf16[256,128]{1,0:T(8,128)(2,1)S(1)} %copy-done), channel_id=1, source_target_pairs={{8,0},{16,8},{24,16},{32,24},{40,32},{48,40},{56,48},{64,56},{72,6... | collective-permute-start | bytes 196616 | tf_op jit(solution)/shard_map/ppermute | solution.py:17
where the time goes:
time: 154 us; the launch traced here: 153 us
  starting transfers between devices  110 us (71%)
  blocking collectives  17.9 us (12%)
  waiting for transfers between devices  9.34 us (6%)
  matrix products  9.3 us (6%)
  local copies, waits for them, and re-layouts  3.39 us (2%)
  other arithmetic  2.16 us (1%)
    ppermute x20, starting transfers between devices, shifted(): return lax.ppermute(block, axis, route)  103 us
    all_to_all x1, blocking collectives, shards(): lax.all_to_all(context, 'head', split_axis=0, concat_axis=1, tiled=True)  17.9 us
    ppermute x20, waiting for transfers between devices, shifted(): return lax.ppermute(block, axis, route)  9.34 us
    all_to_all x1, starting transfers between devices, shards(): lax.all_to_all(queries, 'head', split_axis=1, concat_axis=0, tiled=True)  6.71 us
    dot_general x11, matrix products, absorb(): jnp.einsum('rjgk,kjd->rjgd', rounded, value_heads, preferred_element_type...  5.94 us
    dot_general x11, matrix products, absorb(): jnp.einsum('rjgd,kjd->rjgk', grouped, key_heads, preferred_element_type=j...  3.37 us
  transfers between devices with their start and end apart: 21, of which 1 were waited for; matrix products, arithmetic and copies ran while one was open for 6% of the time, Pallas kernels for 0%

commit v1 on v0

v1 whole, which is shorter than its diff:
```python
import functools
import math

import jax
import jax.numpy as jnp
from jax import lax
from jax.experimental import pallas as pl
from jax.experimental.pallas import tpu as pltpu
from jax.sharding import PartitionSpec as P

HEADS = 64
KV_HEADS = 8
HEAD_DIM = 128
MESH = pl.DeviceIdType.MESH
GROUP = HEADS // KV_HEADS
RATE = math.log2(math.e) / math.sqrt(HEAD_DIM)
FAR = 1e30

OWN = {0: 0, -1: 1, 1: 2, -2: 3, 2: 4}
PAIR = {0: 5, -1: 6, 1: 7, -2: 8, 2: 9}
EDGE, SLOTS = 10, 11


class Move:
    def __init__(self, copies, arrives):
        self.copies, self.arrives = copies, arrives

    def start(self):
        for sends, copy in self.copies:
            pl.when(sends)(copy.start)

    def wait_recv(self):
        pl.when(self.arrives)(self.copies[0][1].wait_recv)

    def wait_send(self):
        for sends, copy in self.copies:
            pl.when(sends)(copy.wait_send)


def kernel(
    groups, q_hbm, k_hbm, v_hbm, first_hbm, last_hbm, out_ref, first_ref, last_ref,
    q_buf, k_buf, v_buf, v_rows, total, peak, first, last, ready,
    local_sem, q_send, q_recv, k_send, k_recv, v_send, v_recv, o_send, o_recv,
):
    t = lax.axis_index("tm")
    h = lax.axis_index("head")
    pair, parity = t // 2, t % 2
    side = 1 - 2 * parity
    x, z = pair % 4, pair // 4
    chip, core = h // 2, h % 2
    rows, width = q_buf.shape[1:]
    tokens = k_buf.shape[1]

    opposite_x = {"tm": 8 * z + 2 * ((x + 2) % 4) + parity, "head": h}

    def at_pair(distance):
        return {"tm": (t + groups + 2 * distance) % groups, "head": h}

    def flip(value):
        return value + 1 - 2 * (value % 2)

    def chunk_of(ring):
        start = chip if ring < 2 else (chip + 2) % 4
        return start if ring % 2 == 0 else flip(start)

    def columns(head):
        return pl.ds(pl.multiple_of(head * width, width), width)

    def remote(source, target, send, recv, device):
        return pltpu.make_async_remote_copy(
            source, target, send, recv, device_id=device, device_id_type=MESH
        )

    def head_of(ring, other):
        return 2 * chunk_of(ring) + (core if other == 0 else 1 - core)

    near = [(1, 0), (1, 1), (0, 1)]
    distant = [(2, 0), (2, 1), (3, 0), (3, 1)]
    mates = distant + near

    def q_copy(ring, other):
        target = head_of(ring, other)
        index = 2 * ring + other
        return remote(
            q_hbm.at[:, columns(target)], q_buf.at[h], q_send.at[index], q_recv.at[index],
            {"tm": t, "head": target},
        )

    def k_copy(source, target, role, device):
        return remote(source, target, k_send.at[role], k_recv.at[role], device)

    def v_copy(source, target, role, device):
        return remote(source, target, v_send.at[role], v_recv.at[role], device)

    k_load = pltpu.make_async_copy(k_hbm, k_buf.at[OWN[0]], local_sem.at[0])
    v_load = pltpu.make_async_copy(v_hbm, v_rows, local_sem.at[1])
    q_load = pltpu.make_async_copy(q_hbm.at[:, columns(h)], q_buf.at[h], local_sem.at[2])
    span_loads = [
        pltpu.make_async_copy(first_hbm, first_ref, local_sem.at[4]),
        pltpu.make_async_copy(last_hbm, last_ref, local_sem.at[5]),
    ]
    pairs = groups // 2
    at_start, at_end = z == 0, z == pairs // 4 - 1

    def has(distance):
        return (pair >= -distance) if distance < 0 else (pair < pairs - distance)

    barrier = pltpu.get_barrier_semaphore()
    everywhere = [{"tm": t + side, "head": h}, opposite_x]
    everywhere += [{"tm": t, "head": head_of(*mate)} for mate in mates]
    for partner in everywhere:
        pl.semaphore_signal(barrier, inc=1, device_id=partner, device_id_type=MESH)
    answers = len(everywhere)
    corner = jnp.where(parity == 0, pair == 0, pair == pairs - 1)
    cornered = jnp.where(parity == 0, pair == 3, pair == pairs - 4)
    others = [(has(distance), at_pair(distance)) for distance in (1, -1, 4, -4)]
    others += [(corner, at_pair(3 * side)), (cornered, at_pair(-3 * side))]
    for present, partner in others:
        answers = answers + jnp.where(present, 1, 0)

        @pl.when(present)
        def _(partner=partner):
            pl.semaphore_signal(barrier, inc=1, device_id=partner, device_id_type=MESH)

    for load in (v_load, k_load, *span_loads, q_load):
        load.start()

    low = x < 2
    to_next, to_last = jnp.logical_not(at_end), jnp.logical_not(at_start)

    def pick(base, condition, distance):
        return jnp.where(condition, base[distance], base[-distance])

    def spread(copy, buf, base, role, source):
        moves = {
            e: Move(
                [(has(e), copy(source, buf.at[base[-e]], role + i, at_pair(e)))],
                has(-e),
            )
            for i, e in enumerate((1, -1))
        }
        moves["x"] = copy(source, buf.at[pick(base, low, -2)], role + 2, opposite_x)
        along = copy(
            buf.at[pick(base, low, 2)], buf.at[pick(base, low, -2)], role + 3,
            at_pair(jnp.where(low, 4, -4)),
        )
        moves["z"] = Move(
            [(jnp.where(low, to_next, to_last), along)], jnp.where(low, to_last, to_next)
        )
        return moves

    def edge(copy, buf):
        up = parity == 0
        along = copy(
            buf.at[pick(PAIR, up, 1)], buf.at[EDGE], 9, at_pair(4 * side)
        )
        direct = copy(buf.at[PAIR[0]], buf.at[EDGE], 9, at_pair(3 * side))
        return Move(
            [(jnp.where(up, to_next, to_last), along), (corner, direct)],
            jnp.where(up, to_last | (x == 3), to_next | (x == 0)),
        )

    across = {"tm": t + side, "head": h}
    k_pair = k_copy(k_hbm, k_buf.at[PAIR[0]], 0, across)
    v_pair = v_copy(v_buf.at[OWN[0]], v_buf.at[PAIR[0]], 0, across)
    k_own = spread(k_copy, k_buf, OWN, 1, k_hbm)
    v_own = spread(v_copy, v_buf, OWN, 1, v_buf.at[OWN[0]])
    k_other = spread(k_copy, k_buf, PAIR, 5, k_buf.at[PAIR[0]])
    v_other = spread(v_copy, v_buf, PAIR, 5, v_buf.at[PAIR[0]])
    k_edge, v_edge = edge(k_copy, k_buf), edge(v_copy, v_buf)
    q_moves = {mate: q_copy(*mate) for mate in mates}

    pl.semaphore_wait(barrier, answers)

    first_steps = (1, -1, "x")
    k_pair.start()
    for step in first_steps:
        k_own[step].start()
    q_moves[0, 1].start()
    v_load.wait()
    v_buf[OWN[0]] = v_rows[...].T
    k_pair.wait_send()
    v_pair.start()
    for step in first_steps:
        v_own[step].start()

    unused = [(base[d], jnp.logical_not(has(d))) for base in (OWN, PAIR) for d in (1, -1, 2, -2)]
    unused.append((EDGE, jnp.logical_not(jnp.where(parity == 0, has(-3), has(3)))))
    for slot, empty in unused:
        @pl.when(empty)
        def _(slot=slot):
            k_buf[slot] = jnp.zeros(k_buf.shape[1:], k_buf.dtype)
            v_buf[slot] = jnp.zeros(v_buf.shape[1:], v_buf.dtype)

    for load in span_loads:
        load.wait()
    lane = lax.broadcasted_iota(jnp.int32, (128, 256), 1)
    row = lax.broadcasted_iota(jnp.int32, (128, 256), 0)
    for c in range(4):
        wanted = c * 32 + (lane // 128) * 16 + lane % 16
        chosen = jnp.where(row == wanted, 1.0, 0.0).astype(jnp.bfloat16)
        for ref, held in ((first_ref, first), (last_ref, last)):
            offset_row = (ref[...] - t).astype(jnp.float32)
            offset_row = jnp.broadcast_to(offset_row, (16, 128)).astype(jnp.bfloat16)
            placed = jnp.dot(offset_row, chosen, preferred_element_type=jnp.float32)
            held[c] = placed[0:1]

    def offset(slot):
        for base, shift in ((OWN, 0), (PAIR, side)):
            for distance, index in base.items():
                if index == slot:
                    return 2 * distance + shift
        return -5 * side

    def absorb(c, start, stop, fresh):
        queries = jnp.concatenate(
            [
                q_buf[2 * c + b, :, g * HEAD_DIM:(g + 1) * HEAD_DIM]
                for b in range(2)
                for g in range(GROUP)
            ],
            axis=0,
        )
        begin, finish = first[c], last[c]
        keys = k_buf[start:stop].reshape((stop - start) * tokens, HEAD_DIM)
        scores = lax.dot_general(
            keys, queries, (((1,), (1,)), ((), ())), preferred_element_type=jnp.float32
        )
        scores = [scores[i * tokens:(i + 1) * tokens] for i in range(stop - start)]
        inside, best = [], []
        for slot, score in zip(range(start, stop), scores):
            place = jnp.asarray(offset(slot), jnp.int32).astype(jnp.float32)
            within = (begin <= place) & (place <= finish)
            inside.append(within)
            best.append(jnp.where(within, jnp.max(score, axis=0, keepdims=True), -FAR))
        top = functools.reduce(jnp.maximum, best)
        if not fresh:
            before = peak[c]
            top = jnp.maximum(before, top)
        peak[c] = top
        weights = [
            jnp.exp2((score - jnp.where(within, top, FAR)) * RATE).astype(jnp.bfloat16)
            for score, within in zip(scores, inside)
        ]
        weights = jnp.concatenate(weights, axis=0)
        left = jnp.concatenate([v_buf[slot] for slot in range(start, stop)], axis=1)
        ones = jnp.ones((16, left.shape[1]), jnp.bfloat16)
        left = jnp.concatenate([left, ones], axis=0)
        gained = jnp.dot(left, weights, preferred_element_type=jnp.float32)
        if not fresh:
            gained = gained + total[c] * jnp.exp2((before - top) * RATE)
        return gained

    def visit(rings, start, stop, fresh):
        for ring in rings:
            c = chunk_of(ring)
            total[c] = absorb(c, start, stop, fresh)

    def visit_all(begin, count, start, stop, fresh):
        def body(i, carry):
            c = (begin + 2 * (i // 2)) % 4
            c = c + (i % 2) * (1 - 2 * (c % 2))
            total[c] = absorb(c, start, stop, fresh)
            return carry

        lax.fori_loop(0, count, body, 0)

    k_own["x"].wait_recv()
    k_own["z"].start()
    k_pair.wait_recv()
    for step in ("x", 1, -1):
        k_other[step].start()
    v_pair.wait_send()
    for mate in ((1, 0), (1, 1), (2, 0), (2, 1)):
        q_moves[mate].start()
    v_own["x"].wait_recv()
    v_own["z"].start()
    v_pair.wait_recv()
    for step in ("x", 1, -1):
        v_other[step].start()
    for mate in distant[2:]:
        q_moves[mate].start()
    k_load.wait()
    q_load.wait()
    for step in (1, -1, "z"):
        k_own[step].wait_recv()
        v_own[step].wait_recv()
    q_moves[0, 1].wait_recv()
    visit((0,), 0, 6, True)

    k_other["x"].wait_recv()
    k_other["z"].start()
    k_other[1].wait_recv()
    k_other[-1].wait_recv()
    k_edge.start()
    q_moves[1, 0].wait_recv()
    q_moves[1, 1].wait_recv()
    visit((1,), 0, 6, True)

    v_other["x"].wait_recv()
    v_other["z"].start()
    v_other[1].wait_recv()
    v_other[-1].wait_recv()
    v_edge.start()
    for mate in distant[:2]:
        q_moves[mate].wait_recv()
    visit((2,), 0, 6, True)
    for mate in distant[2:]:
        q_moves[mate].wait_recv()
    visit((3,), 0, 6, True)
    visit_all(chip, 4, 6, 8, False)

    for move in (k_other["z"], v_other["z"], k_edge, v_edge):
        move.wait_recv()

    own_out = pltpu.make_async_copy(ready.at[h], out_ref.at[:, columns(h)], local_sem.at[3])

    def o_copy(ring, other):
        target = head_of(ring, other)
        index = 2 * ring + other
        return remote(
            ready.at[target], out_ref.at[:, columns(h)], o_send.at[index], o_recv.at[index],
            {"tm": t, "head": target},
        )

    o_moves = {mate: o_copy(*mate) for mate in mates}
    for ring in (3, 2, 1, 0):
        c = chunk_of(ring)
        done = absorb(c, 8, 11, False)
        mean = done[:HEAD_DIM] / done[HEAD_DIM:HEAD_DIM + 1]
        turned = mean.T.astype(jnp.bfloat16)
        for b in range(2):
            for g in range(GROUP):
                begin = (b * GROUP + g) * rows
                ready[2 * c + b, :, g * HEAD_DIM:(g + 1) * HEAD_DIM] = turned[begin:begin + rows]
        for mate in mates:
            if mate[0] == ring:
                o_moves[mate].start()
        if ring == 0:
            own_out.start()

    for moves in (k_own, v_own, k_other, v_other):
        for move in moves.values():
            move.wait_send()
    k_edge.wait_send()
    v_edge.wait_send()
    for move in q_moves.values():
        move.wait_send()
    own_out.wait()
    for move in o_moves.values():
        move.wait_recv()
        move.wait_send()


def shards(groups, queries, vis_keys, vis_values, span_start, span_end):
    rows, width = queries.shape
    tokens = vis_keys.shape[0]
    part = width // KV_HEADS
    dma = pltpu.SemaphoreType.DMA
    spans = [span.reshape(1, -1) for span in (span_start, span_end)]
    operands = [queries, vis_keys, vis_values, *spans]
    flops = 4 * rows * width * tokens * SLOTS
    return pl.pallas_call(
        functools.partial(kernel, groups),
        out_shape=pltpu.VMEM((rows, width), jnp.bfloat16),
        in_specs=[pl.BlockSpec(memory_space=pltpu.HBM)] * 5,
        out_specs=pl.BlockSpec(memory_space=pl.ANY),
        scratch_shapes=[
            pltpu.VMEM(spans[0].shape, jnp.int32),
            pltpu.VMEM(spans[1].shape, jnp.int32),
            pltpu.VMEM((KV_HEADS, rows, part), jnp.bfloat16),
            pltpu.VMEM((SLOTS, tokens, HEAD_DIM), jnp.bfloat16),
            pltpu.VMEM((SLOTS, HEAD_DIM, tokens), jnp.bfloat16),
            pltpu.VMEM((tokens, HEAD_DIM), jnp.bfloat16),
            pltpu.VMEM((4, HEAD_DIM + 16, 256), jnp.float32),
            pltpu.VMEM((4, 1, 256), jnp.float32),
            pltpu.VMEM((4, 1, 256), jnp.float32),
            pltpu.VMEM((4, 1, 256), jnp.float32),
            pltpu.VMEM((KV_HEADS, rows, part), jnp.bfloat16),
            dma((6,)),
            dma((8,)),
            dma((8,)),
            dma((10,)),
            dma((10,)),
            dma((10,)),
            dma((10,)),
            dma((8,)),
            dma((8,)),
        ],
        cost_estimate=pl.CostEstimate(
            flops=flops, bytes_accessed=8 * rows * width, transcendentals=flops // 512
        ),
        compiler_params=pltpu.CompilerParams(
            collective_id=0, has_side_effects=True, vmem_limit_bytes=40 * 1024 * 1024
        ),
    )(*[pltpu.with_memory_space_constraint(value, pltpu.HBM) for value in operands])


def solution(mesh):
    return jax.shard_map(
        functools.partial(shards, mesh.shape["tm"]),
        mesh=mesh,
        in_specs=(P(("tm", "head"), None), P("tm", "head"), P("tm", "head"), P("tm"), P("tm")),
        out_specs=P(("tm", "head"), None),
        check_vma=False,
    )
```

time: 154 us -> 36.4 us (0.24)
  the two profiles are of different devices: /device:TPU:255 before, /device:TPU:135 now
where the time goes in v1:
time: 36.4 us; the launch traced here: 36.3 us
  Pallas kernels  35.5 us (98%)
  local copies, waits for them, and re-layouts  0.71 us (2%)
    pallas_call x1, Pallas kernels, shards(): pl.pallas_call(functools.partial(kernel, groups), out_shape=pltpu.VMEM((r...  35.5 us

profile of v1, /device:TPU:135, one launch (start us, length us, event | category | flops | bytes accessed | tf_op | source)
XLA Modules:
  0.0 36.3 jit_solution(15276978146018259309)
XLA Ops:
  0.0 35.5 %shard_map.55 = bf16[16,8192]{1,0:T(8,128)(2,1)S(1)} custom-call(bf16[16,8192]{1,0:T(8,128)(2,1)} %q_hbm.1, bf16[256,128]{1,0:T(8,128)(2,1)} %k_hbm.1, bf16[256,128]{1,0:T(8,128)(2,1)} %v_hbm.1, s32[1,128]{1,0:T(1,128)} %bitcast.2, s32[1,128]{1,0:T(1,128)} %bitcast.3), custom_call_target="tpu_custom_call" | custom-call | flops 1476395008 | bytes 1048576 | tf_op jit(solution)/shard_map/pallas_call | solution.py:363
  35.5 0.7 %copy.7 = bf16[16,8192]{1,0:T(8,128)(2,1)} copy(bf16[16,8192]{1,0:T(8,128)(2,1)S(1)} %shard_map.55) | data formatting | bytes 524288

commit v2 on v1

--- a/solution.py
+++ b/solution.py
@@ -39,7 +39,7 @@
 
 def kernel(
     groups, q_hbm, k_hbm, v_hbm, first_hbm, last_hbm, out_ref, first_ref, last_ref,
-    q_buf, k_buf, v_buf, v_rows, total, peak, first, last, ready,
+    q_buf, k_buf, v_buf, k_relay, v_relay, v_rows, total, peak, first, last, ready,
     local_sem, q_send, q_recv, k_send, k_recv, v_send, v_recv, o_send, o_recv,
 ):
     t = lax.axis_index("tm")
@@ -56,6 +56,10 @@
     def at_pair(distance):
         return {"tm": (t + groups + 2 * distance) % groups, "head": h}
 
+    def along_y(distance):
+        there = (4 * parity + chip + 8 + distance) % 8
+        return {"tm": 2 * pair + there // 4, "head": 2 * (there % 4) + core}
+
     def flip(value):
         return value + 1 - 2 * (value % 2)
 
@@ -106,7 +110,7 @@
         return (pair >= -distance) if distance < 0 else (pair < pairs - distance)
 
     barrier = pltpu.get_barrier_semaphore()
-    everywhere = [{"tm": t + side, "head": h}, opposite_x]
+    everywhere = [along_y(2), along_y(-2), opposite_x]
     everywhere += [{"tm": t, "head": head_of(*mate)} for mate in mates]
     for partner in everywhere:
         pl.semaphore_signal(barrier, inc=1, device_id=partner, device_id_type=MESH)
@@ -160,9 +164,22 @@
             jnp.where(up, to_last | (x == 3), to_next | (x == 0)),
         )
 
-    across = {"tm": t + side, "head": h}
-    k_pair = k_copy(k_hbm, k_buf.at[PAIR[0]], 0, across)
-    v_pair = v_copy(v_buf.at[OWN[0]], v_buf.at[PAIR[0]], 0, across)
+    def legs(copy, buf, source, passing):
+        half = passing.shape[0] // 2
+        parts = ((pl.ds(0, half), 2, 0, 11), (pl.ds(half, half), -2, 10, 12))
+        return [
+            [
+                copy(source.at[part], passing.at[part], role, along_y(way))
+                for part, way, role, _ in parts
+            ],
+            [
+                copy(passing.at[part], buf.at[PAIR[0], part], role, along_y(way))
+                for part, way, _, role in parts
+            ],
+        ]
+
+    k_leg = legs(k_copy, k_buf, k_hbm, k_relay)
+    v_leg = legs(v_copy, v_buf, v_buf.at[OWN[0]], v_relay)
     k_own = spread(k_copy, k_buf, OWN, 1, k_hbm)
     v_own = spread(v_copy, v_buf, OWN, 1, v_buf.at[OWN[0]])
     k_other = spread(k_copy, k_buf, PAIR, 5, k_buf.at[PAIR[0]])
@@ -173,16 +190,21 @@
     pl.semaphore_wait(barrier, answers)
 
     first_steps = (1, -1, "x")
-    k_pair.start()
+    for move in k_leg[0]:
+        move.start()
     for step in first_steps:
         k_own[step].start()
     q_moves[0, 1].start()
     v_load.wait()
     v_buf[OWN[0]] = v_rows[...].T
-    k_pair.wait_send()
-    v_pair.start()
+    for move in k_leg[0]:
+        move.wait_send()
+    for move in v_leg[0]:
+        move.start()
     for step in first_steps:
         v_own[step].start()
+    for mate in ((1, 0), (1, 1)):
+        q_moves[mate].start()
 
     unused = [(base[d], jnp.logical_not(has(d))) for base in (OWN, PAIR) for d in (1, -1, 2, -2)]
     unused.append((EDGE, jnp.logical_not(jnp.where(parity == 0, has(-3), has(3)))))
@@ -265,46 +287,55 @@
 
         lax.fori_loop(0, count, body, 0)
 
+    for move, onward in zip(k_leg[0], k_leg[1]):
+        move.wait_recv()
+        onward.start()
     k_own["x"].wait_recv()
     k_own["z"].start()
-    k_pair.wait_recv()
+    for move, onward in zip(v_leg[0], v_leg[1]):
+        move.wait_recv()
+        onward.start()
+    for mate in distant[:2]:
+        q_moves[mate].start()
+    for move in k_leg[1]:
+        move.wait_recv()
     for step in ("x", 1, -1):
         k_other[step].start()
-    v_pair.wait_send()
-    for mate in ((1, 0), (1, 1), (2, 0), (2, 1)):
-        q_moves[mate].start()
     v_own["x"].wait_recv()
     v_own["z"].start()
-    v_pair.wait_recv()
+    k_load.wait()
+    q_load.wait()
+    for step in (1, -1):
+        k_own[step].wait_recv()
+        v_own[step].wait_recv()
+    for mate in near:
+        q_moves[mate].wait_recv()
+    visit_all(chip, 2, 0, 3, True)
+
+    for move in v_leg[1]:
+        move.wait_recv()
     for step in ("x", 1, -1):
         v_other[step].start()
     for mate in distant[2:]:
         q_moves[mate].start()
-    k_load.wait()
-    q_load.wait()
-    for step in (1, -1, "z"):
-        k_own[step].wait_recv()
-        v_own[step].wait_recv()
-    q_moves[0, 1].wait_recv()
-    visit((0,), 0, 6, True)
+    k_own["z"].wait_recv()
+    v_own["z"].wait_recv()
+    visit_all(chip, 2, 3, 6, False)
 
     k_other["x"].wait_recv()
     k_other["z"].start()
     k_other[1].wait_recv()
     k_other[-1].wait_recv()
     k_edge.start()
-    q_moves[1, 0].wait_recv()
-    q_moves[1, 1].wait_recv()
-    visit((1,), 0, 6, True)
+    for mate in distant[:2]:
+        q_moves[mate].wait_recv()
+    visit((2,), 0, 6, True)
 
     v_other["x"].wait_recv()
     v_other["z"].start()
     v_other[1].wait_recv()
     v_other[-1].wait_recv()
     v_edge.start()
-    for mate in distant[:2]:
-        q_moves[mate].wait_recv()
-    visit((2,), 0, 6, True)
     for mate in distant[2:]:
         q_moves[mate].wait_recv()
     visit((3,), 0, 6, True)
@@ -342,8 +373,8 @@
     for moves in (k_own, v_own, k_other, v_other):
         for move in moves.values():
             move.wait_send()
-    k_edge.wait_send()
-    v_edge.wait_send()
+    for move in (k_edge, v_edge, *k_leg[1], *v_leg[0], *v_leg[1]):
+        move.wait_send()
     for move in q_moves.values():
         move.wait_send()
     own_out.wait()
@@ -372,6 +403,8 @@
             pltpu.VMEM((SLOTS, tokens, HEAD_DIM), jnp.bfloat16),
             pltpu.VMEM((SLOTS, HEAD_DIM, tokens), jnp.bfloat16),
             pltpu.VMEM((tokens, HEAD_DIM), jnp.bfloat16),
+            pltpu.VMEM((HEAD_DIM, tokens), jnp.bfloat16),
+            pltpu.VMEM((tokens, HEAD_DIM), jnp.bfloat16),
             pltpu.VMEM((4, HEAD_DIM + 16, 256), jnp.float32),
             pltpu.VMEM((4, 1, 256), jnp.float32),
             pltpu.VMEM((4, 1, 256), jnp.float32),
@@ -380,10 +413,10 @@
             dma((6,)),
             dma((8,)),
             dma((8,)),
-            dma((10,)),
-            dma((10,)),
-            dma((10,)),
-            dma((10,)),
+            dma((13,)),
+            dma((13,)),
+            dma((13,)),
+            dma((13,)),
             dma((8,)),
             dma((8,)),
         ],

time: 36.4 us -> 36.6 us (level)
  the two profiles are of different devices: /device:TPU:135 before, /device:TPU:1 now
where the time goes in v2:
time: 36.6 us; the launch traced here: 36.4 us
  Pallas kernels  35.7 us (98%)
  local copies, waits for them, and re-layouts  0.71 us (2%)
    pallas_call x1, Pallas kernels, shards(): pl.pallas_call(functools.partial(kernel, groups), out_shape=pltpu.VMEM((r...  35.7 us

profile of v2, /device:TPU:1, one launch (start us, length us, event | category | flops | bytes accessed | tf_op | source)
XLA Modules:
  0.0 36.4 jit_solution(3517567955742802079)
XLA Ops:
  0.0 35.7 %shard_map.55 = bf16[16,8192]{1,0:T(8,128)(2,1)S(1)} custom-call(bf16[16,8192]{1,0:T(8,128)(2,1)} %q_hbm.1, bf16[256,128]{1,0:T(8,128)(2,1)} %k_hbm.1, bf16[256,128]{1,0:T(8,128)(2,1)} %v_hbm.1, s32[1,128]{1,0:T(1,128)} %bitcast.2, s32[1,128]{1,0:T(1,128)} %bitcast.3), custom_call_target="tpu_custom_call" | custom-call | flops 1476395008 | bytes 1048576 | tf_op jit(solution)/shard_map/pallas_call | solution.py:394
  35.7 0.7 %copy.7 = bf16[16,8192]{1,0:T(8,128)(2,1)} copy(bf16[16,8192]{1,0:T(8,128)(2,1)S(1)} %shard_map.55) | data formatting | bytes 524288

commit v3 on v2

--- a/solution.py
+++ b/solution.py
@@ -218,14 +218,14 @@
         load.wait()
     lane = lax.broadcasted_iota(jnp.int32, (128, 256), 1)
     row = lax.broadcasted_iota(jnp.int32, (128, 256), 0)
-    for c in range(4):
-        wanted = c * 32 + (lane // 128) * 16 + lane % 16
+    for ring in range(4):
+        wanted = chunk_of(ring) * 32 + (lane // 128) * 16 + lane % 16
         chosen = jnp.where(row == wanted, 1.0, 0.0).astype(jnp.bfloat16)
         for ref, held in ((first_ref, first), (last_ref, last)):
             offset_row = (ref[...] - t).astype(jnp.float32)
             offset_row = jnp.broadcast_to(offset_row, (16, 128)).astype(jnp.bfloat16)
             placed = jnp.dot(offset_row, chosen, preferred_element_type=jnp.float32)
-            held[c] = placed[0:1]
+            held[ring] = placed[0:1]
 
     def offset(slot):
         for base, shift in ((OWN, 0), (PAIR, side)):
@@ -234,58 +234,55 @@
                     return 2 * distance + shift
         return -5 * side
 
-    def absorb(c, start, stop, fresh):
+    def score(ring, slot):
         queries = jnp.concatenate(
             [
-                q_buf[2 * c + b, :, g * HEAD_DIM:(g + 1) * HEAD_DIM]
+                q_buf[2 * chunk_of(ring) + b, :, g * HEAD_DIM:(g + 1) * HEAD_DIM]
                 for b in range(2)
                 for g in range(GROUP)
             ],
             axis=0,
         )
-        begin, finish = first[c], last[c]
-        keys = k_buf[start:stop].reshape((stop - start) * tokens, HEAD_DIM)
-        scores = lax.dot_general(
-            keys, queries, (((1,), (1,)), ((), ())), preferred_element_type=jnp.float32
-        )
-        scores = [scores[i * tokens:(i + 1) * tokens] for i in range(stop - start)]
-        inside, best = [], []
-        for slot, score in zip(range(start, stop), scores):
-            place = jnp.asarray(offset(slot), jnp.int32).astype(jnp.float32)
-            within = (begin <= place) & (place <= finish)
-            inside.append(within)
-            best.append(jnp.where(within, jnp.max(score, axis=0, keepdims=True), -FAR))
-        top = functools.reduce(jnp.maximum, best)
-        if not fresh:
-            before = peak[c]
-            top = jnp.maximum(before, top)
-        peak[c] = top
-        weights = [
-            jnp.exp2((score - jnp.where(within, top, FAR)) * RATE).astype(jnp.bfloat16)
-            for score, within in zip(scores, inside)
-        ]
-        weights = jnp.concatenate(weights, axis=0)
-        left = jnp.concatenate([v_buf[slot] for slot in range(start, stop)], axis=1)
-        ones = jnp.ones((16, left.shape[1]), jnp.bfloat16)
-        left = jnp.concatenate([left, ones], axis=0)
-        gained = jnp.dot(left, weights, preferred_element_type=jnp.float32)
-        if not fresh:
-            gained = gained + total[c] * jnp.exp2((before - top) * RATE)
-        return gained
-
-    def visit(rings, start, stop, fresh):
-        for ring in rings:
-            c = chunk_of(ring)
-            total[c] = absorb(c, start, stop, fresh)
-
-    def visit_all(begin, count, start, stop, fresh):
-        def body(i, carry):
-            c = (begin + 2 * (i // 2)) % 4
-            c = c + (i % 2) * (1 - 2 * (c % 2))
-            total[c] = absorb(c, start, stop, fresh)
-            return carry
-
-        lax.fori_loop(0, count, body, 0)
+        return lax.dot_general(
+            k_buf[slot], queries, (((1,), (1,)), ((), ())), preferred_element_type=jnp.float32
+        )
+
+    def visit(units, fresh=False, finish=None):
+        scores = [score(units[0][0], slot) for slot in units[0][1]]
+        ones = jnp.ones((16, tokens), jnp.bfloat16)
+        for at, (ring, slots) in enumerate(units):
+            following = units[at + 1] if at + 1 < len(units) else (ring, ())
+            renew = fresh and all(ring != earlier for earlier, _ in units[:at])
+            begin, end = first[ring], last[ring]
+            inside, best = [], []
+            for slot, part in zip(slots, scores):
+                place = jnp.asarray(offset(slot), jnp.int32).astype(jnp.float32)
+                within = (begin <= place) & (place <= end)
+                inside.append(within)
+                best.append(jnp.where(within, jnp.max(part, axis=0, keepdims=True), -FAR))
+            top = functools.reduce(jnp.maximum, best)
+            if renew:
+                gained = jnp.zeros(total.shape[1:], jnp.float32)
+            else:
+                before = peak[ring]
+                top = jnp.maximum(before, top)
+                gained = total[ring] * jnp.exp2((before - top) * RATE)
+            ahead = []
+            for i, slot in enumerate(slots):
+                if i < len(following[1]):
+                    ahead.append(score(following[0], following[1][i]))
+                level = jnp.where(inside[i], top, FAR)
+                weights = jnp.exp2((scores[i] - level) * RATE).astype(jnp.bfloat16)
+                left = jnp.concatenate([v_buf[slot], ones], axis=0)
+                gained = gained + jnp.dot(left, weights, preferred_element_type=jnp.float32)
+            for slot in following[1][len(slots):]:
+                ahead.append(score(following[0], slot))
+            if finish is None:
+                peak[ring] = top
+                total[ring] = gained
+            else:
+                finish(ring, gained)
+            scores = ahead
 
     for move, onward in zip(k_leg[0], k_leg[1]):
         move.wait_recv()
@@ -310,7 +307,7 @@
         v_own[step].wait_recv()
     for mate in near:
         q_moves[mate].wait_recv()
-    visit_all(chip, 2, 0, 3, True)
+    visit([(0, (0, 1, 2)), (1, (0, 1, 2))], fresh=True)
 
     for move in v_leg[1]:
         move.wait_recv()
@@ -320,7 +317,7 @@
         q_moves[mate].start()
     k_own["z"].wait_recv()
     v_own["z"].wait_recv()
-    visit_all(chip, 2, 3, 6, False)
+    visit([(0, (3, 4, 5)), (1, (3, 4, 5))])
 
     k_other["x"].wait_recv()
     k_other["z"].start()
@@ -329,17 +326,17 @@
     k_edge.start()
     for mate in distant[:2]:
         q_moves[mate].wait_recv()
-    visit((2,), 0, 6, True)
+    visit([(2, (0, 1, 2)), (2, (3, 4, 5))], fresh=True)
 
     v_other["x"].wait_recv()
     v_other["z"].start()
     v_other[1].wait_recv()
     v_other[-1].wait_recv()
     v_edge.start()
+    visit([(ring, (6, 7)) for ring in range(3)])
     for mate in distant[2:]:
         q_moves[mate].wait_recv()
-    visit((3,), 0, 6, True)
-    visit_all(chip, 4, 6, 8, False)
+    visit([(3, (0, 1, 2)), (3, (3, 4, 5)), (3, (6, 7))], fresh=True)
 
     for move in (k_other["z"], v_other["z"], k_edge, v_edge):
         move.wait_recv()
@@ -355,20 +352,22 @@
         )
 
     o_moves = {mate: o_copy(*mate) for mate in mates}
-    for ring in (3, 2, 1, 0):
-        c = chunk_of(ring)
-        done = absorb(c, 8, 11, False)
+    def send(ring, done):
         mean = done[:HEAD_DIM] / done[HEAD_DIM:HEAD_DIM + 1]
         turned = mean.T.astype(jnp.bfloat16)
         for b in range(2):
             for g in range(GROUP):
                 begin = (b * GROUP + g) * rows
-                ready[2 * c + b, :, g * HEAD_DIM:(g + 1) * HEAD_DIM] = turned[begin:begin + rows]
+                ready[2 * chunk_of(ring) + b, :, g * HEAD_DIM:(g + 1) * HEAD_DIM] = turned[
+                    begin:begin + rows
+                ]
         for mate in mates:
             if mate[0] == ring:
                 o_moves[mate].start()
         if ring == 0:
             own_out.start()
+
+    visit([(ring, (8, 9, 10)) for ring in (3, 2, 1, 0)], finish=send)
 
     for moves in (k_own, v_own, k_other, v_other):
         for move in moves.values():

time: 36.6 us -> 35.4 us (0.967)
  the two profiles are of different devices: /device:TPU:1 before, /device:TPU:135 now
where the time goes in v3:
time: 35.4 us; the launch traced here: 35.3 us
  Pallas kernels  34.6 us (98%)
  local copies, waits for them, and re-layouts  0.71 us (2%)
    pallas_call x1, Pallas kernels, shards(): pl.pallas_call(functools.partial(kernel, groups), out_shape=pltpu.VMEM((r...  34.6 us

profile of v3, /device:TPU:135, one launch (start us, length us, event | category | flops | bytes accessed | tf_op | source)
XLA Modules:
  0.0 35.3 jit_solution(17597197065654088100)
XLA Ops:
  0.0 34.6 %shard_map.55 = bf16[16,8192]{1,0:T(8,128)(2,1)S(1)} custom-call(bf16[16,8192]{1,0:T(8,128)(2,1)} %q_hbm.1, bf16[256,128]{1,0:T(8,128)(2,1)} %k_hbm.1, bf16[256,128]{1,0:T(8,128)(2,1)} %v_hbm.1, s32[1,128]{1,0:T(1,128)} %bitcast.2, s32[1,128]{1,0:T(1,128)} %bitcast.3), custom_call_target="tpu_custom_call" | custom-call | flops 1476395008 | bytes 1048576 | tf_op jit(solution)/shard_map/pallas_call | solution.py:393
  34.6 0.7 %copy.7 = bf16[16,8192]{1,0:T(8,128)(2,1)} copy(bf16[16,8192]{1,0:T(8,128)(2,1)S(1)} %shard_map.55) | data formatting | bytes 524288

commit v4 on v3

--- a/solution.py
+++ b/solution.py
@@ -16,8 +16,8 @@
 RATE = math.log2(math.e) / math.sqrt(HEAD_DIM)
 FAR = 1e30
 
-OWN = {0: 0, -1: 1, 1: 2, -2: 3, 2: 4}
-PAIR = {0: 5, -1: 6, 1: 7, -2: 8, 2: 9}
+OWN = {0: 0, -1: 1, 1: 2, "x": 3, "z": 4}
+PAIR = {0: 5, -1: 6, 1: 7, "x": 8, "z": 9}
 EDGE, SLOTS = 10, 11
 
 
@@ -132,9 +132,6 @@
     low = x < 2
     to_next, to_last = jnp.logical_not(at_end), jnp.logical_not(at_start)
 
-    def pick(base, condition, distance):
-        return jnp.where(condition, base[distance], base[-distance])
-
     def spread(copy, buf, base, role, source):
         moves = {
             e: Move(
@@ -143,10 +140,9 @@
             )
             for i, e in enumerate((1, -1))
         }
-        moves["x"] = copy(source, buf.at[pick(base, low, -2)], role + 2, opposite_x)
+        moves["x"] = copy(source, buf.at[base["x"]], role + 2, opposite_x)
         along = copy(
-            buf.at[pick(base, low, 2)], buf.at[pick(base, low, -2)], role + 3,
-            at_pair(jnp.where(low, 4, -4)),
+            buf.at[base["x"]], buf.at[base["z"]], role + 3, at_pair(jnp.where(low, 4, -4))
         )
         moves["z"] = Move(
             [(jnp.where(low, to_next, to_last), along)], jnp.where(low, to_last, to_next)
@@ -155,9 +151,8 @@
 
     def edge(copy, buf):
         up = parity == 0
-        along = copy(
-            buf.at[pick(PAIR, up, 1)], buf.at[EDGE], 9, at_pair(4 * side)
-        )
+        beside = jnp.where(up, PAIR[1], PAIR[-1])
+        along = copy(buf.at[beside], buf.at[EDGE], 9, at_pair(4 * side))
         direct = copy(buf.at[PAIR[0]], buf.at[EDGE], 9, at_pair(3 * side))
         return Move(
             [(jnp.where(up, to_next, to_last), along), (corner, direct)],
@@ -206,7 +201,8 @@
     for mate in ((1, 0), (1, 1)):
         q_moves[mate].start()
 
-    unused = [(base[d], jnp.logical_not(has(d))) for base in (OWN, PAIR) for d in (1, -1, 2, -2)]
+    unused = [(base[d], jnp.logical_not(has(d))) for base in (OWN, PAIR) for d in (1, -1)]
+    unused += [(base["z"], jnp.where(low, at_start, at_end)) for base in (OWN, PAIR)]
     unused.append((EDGE, jnp.logical_not(jnp.where(parity == 0, has(-3), has(3)))))
     for slot, empty in unused:
         @pl.when(empty)
@@ -228,10 +224,11 @@
             held[ring] = placed[0:1]
 
     def offset(slot):
+        places = {"x": jnp.where(low, 2, -2), "z": jnp.where(low, -2, 2)}
         for base, shift in ((OWN, 0), (PAIR, side)):
             for distance, index in base.items():
                 if index == slot:
-                    return 2 * distance + shift
+                    return 2 * places.get(distance, distance) + shift
         return -5 * side
 
     def score(ring, slot):
@@ -307,7 +304,7 @@
         v_own[step].wait_recv()
     for mate in near:
         q_moves[mate].wait_recv()
-    visit([(0, (0, 1, 2)), (1, (0, 1, 2))], fresh=True)
+    visit([(0, (0, 1, 2, 3)), (1, (0, 1, 2, 3))], fresh=True)
 
     for move in v_leg[1]:
         move.wait_recv()
@@ -317,7 +314,7 @@
         q_moves[mate].start()
     k_own["z"].wait_recv()
     v_own["z"].wait_recv()
-    visit([(0, (3, 4, 5)), (1, (3, 4, 5))])
+    visit([(0, (4, 5)), (1, (4, 5))])
 
     k_other["x"].wait_recv()
     k_other["z"].start()
@@ -333,10 +330,10 @@
     v_other[1].wait_recv()
     v_other[-1].wait_recv()
     v_edge.start()
-    visit([(ring, (6, 7)) for ring in range(3)])
+    visit([(ring, (6, 7, 8)) for ring in range(3)])
     for mate in distant[2:]:
         q_moves[mate].wait_recv()
-    visit([(3, (0, 1, 2)), (3, (3, 4, 5)), (3, (6, 7))], fresh=True)
+    visit([(3, (0, 1, 2)), (3, (3, 4, 5)), (3, (6, 7, 8))], fresh=True)
 
     for move in (k_other["z"], v_other["z"], k_edge, v_edge):
         move.wait_recv()
@@ -367,7 +364,7 @@
         if ring == 0:
             own_out.start()
 
-    visit([(ring, (8, 9, 10)) for ring in (3, 2, 1, 0)], finish=send)
+    visit([(ring, (9, 10)) for ring in (3, 2, 1, 0)], finish=send)
 
     for moves in (k_own, v_own, k_other, v_other):
         for move in moves.values():

time: 35.4 us -> 35.2 us (level)
  no operation moved by 1% of the time
where the time goes in v4:
time: 35.2 us; the launch traced here: 35 us
  Pallas kernels  34.3 us (97%)
  local copies, waits for them, and re-layouts  0.71 us (2%)
    pallas_call x1, Pallas kernels, shards(): pl.pallas_call(functools.partial(kernel, groups), out_shape=pltpu.VMEM((r...  34.3 us
    unnamed x1, local copies, waits for them, and re-layouts  0.71 us

profile of v4, /device:TPU:135, one launch (start us, length us, event | category | flops | bytes accessed | tf_op | source)
XLA Modules:
  0.0 35.0 jit_solution(1080982777320261914)
XLA Ops:
  0.0 34.3 %shard_map.55 = bf16[16,8192]{1,0:T(8,128)(2,1)S(1)} custom-call(bf16[16,8192]{1,0:T(8,128)(2,1)} %q_hbm.1, bf16[256,128]{1,0:T(8,128)(2,1)} %k_hbm.1, bf16[256,128]{1,0:T(8,128)(2,1)} %v_hbm.1, s32[1,128]{1,0:T(1,128)} %bitcast.2, s32[1,128]{1,0:T(1,128)} %bitcast.3), custom_call_target="tpu_custom_call" | custom-call | flops 1476395008 | bytes 1048576 | tf_op jit(solution)/shard_map/pallas_call | solution.py:390
  34.3 0.7 %copy.7 = bf16[16,8192]{1,0:T(8,128)(2,1)} copy(bf16[16,8192]{1,0:T(8,128)(2,1)S(1)} %shard_map.55) | data formatting | bytes 524288

commit v5 on v4

--- a/solution.py
+++ b/solution.py
@@ -64,7 +64,7 @@
         return value + 1 - 2 * (value % 2)
 
     def chunk_of(ring):
-        start = chip if ring < 2 else (chip + 2) % 4
+        start = chip if ring < 2 else 3 - chip
         return start if ring % 2 == 0 else flip(start)
 
     def columns(head):
@@ -284,17 +284,19 @@
     for move, onward in zip(k_leg[0], k_leg[1]):
         move.wait_recv()
         onward.start()
+    for mate in distant[:2]:
+        q_moves[mate].start()
     k_own["x"].wait_recv()
     k_own["z"].start()
     for move, onward in zip(v_leg[0], v_leg[1]):
         move.wait_recv()
         onward.start()
-    for mate in distant[:2]:
-        q_moves[mate].start()
     for move in k_leg[1]:
         move.wait_recv()
     for step in ("x", 1, -1):
         k_other[step].start()
+    for mate in distant[2:]:
+        q_moves[mate].start()
     v_own["x"].wait_recv()
     v_own["z"].start()
     k_load.wait()
@@ -310,8 +312,6 @@
         move.wait_recv()
     for step in ("x", 1, -1):
         v_other[step].start()
-    for mate in distant[2:]:
-        q_moves[mate].start()
     k_own["z"].wait_recv()
     v_own["z"].wait_recv()
     visit([(0, (4, 5)), (1, (4, 5))])
@@ -364,7 +364,7 @@
         if ring == 0:
             own_out.start()
 
-    visit([(ring, (9, 10)) for ring in (3, 2, 1, 0)], finish=send)
+    visit([(ring, (9, 10)) for ring in (2, 3, 1, 0)], finish=send)
 
     for moves in (k_own, v_own, k_other, v_other):
         for move in moves.values():

time: 35.2 us -> 36.1 us (1.026)
  the two profiles are of different devices: /device:TPU:135 before, /device:TPU:199 now
where the time goes in v5:
time: 36.1 us; the launch traced here: 35.9 us
  Pallas kernels  35.2 us (98%)
  local copies, waits for them, and re-layouts  0.71 us (2%)
    pallas_call x1, Pallas kernels, shards(): pl.pallas_call(functools.partial(kernel, groups), out_shape=pltpu.VMEM((r...  35.2 us

profile of v5, /device:TPU:199, one launch (start us, length us, event | category | flops | bytes accessed | tf_op | source)
XLA Modules:
  0.0 35.9 jit_solution(13690804747547233051)
XLA Ops:
  0.0 35.2 %shard_map.55 = bf16[16,8192]{1,0:T(8,128)(2,1)S(1)} custom-call(bf16[16,8192]{1,0:T(8,128)(2,1)} %q_hbm.1, bf16[256,128]{1,0:T(8,128)(2,1)} %k_hbm.1, bf16[256,128]{1,0:T(8,128)(2,1)} %v_hbm.1, s32[1,128]{1,0:T(1,128)} %bitcast.2, s32[1,128]{1,0:T(1,128)} %bitcast.3), custom_call_target="tpu_custom_call" | custom-call | flops 1476395008 | bytes 1048576 | tf_op jit(solution)/shard_map/pallas_call | solution.py:390
  35.2 0.7 %copy.7 = bf16[16,8192]{1,0:T(8,128)(2,1)} copy(bf16[16,8192]{1,0:T(8,128)(2,1)S(1)} %shard_map.55) | data formatting | bytes 524288

commit v6 on v4

--- a/solution.py
+++ b/solution.py
@@ -39,7 +39,7 @@
 
 def kernel(
     groups, q_hbm, k_hbm, v_hbm, first_hbm, last_hbm, out_ref, first_ref, last_ref,
-    q_buf, k_buf, v_buf, k_relay, v_relay, v_rows, total, peak, first, last, ready,
+    q_buf, q_turned, k_buf, v_buf, k_relay, v_relay, v_rows, total, peak, first, last, ready,
     local_sem, q_send, q_recv, k_send, k_recv, v_send, v_recv, o_send, o_recv,
 ):
     t = lax.axis_index("tm")
@@ -231,18 +231,16 @@
                     return 2 * places.get(distance, distance) + shift
         return -5 * side
 
+    def turn_queries(ring):
+        queries = [
+            q_buf[2 * chunk_of(ring) + b, :, g * HEAD_DIM:(g + 1) * HEAD_DIM]
+            for b in range(2)
+            for g in range(GROUP)
+        ]
+        q_turned[ring] = jnp.concatenate(queries, axis=0).T
+
     def score(ring, slot):
-        queries = jnp.concatenate(
-            [
-                q_buf[2 * chunk_of(ring) + b, :, g * HEAD_DIM:(g + 1) * HEAD_DIM]
-                for b in range(2)
-                for g in range(GROUP)
-            ],
-            axis=0,
-        )
-        return lax.dot_general(
-            k_buf[slot], queries, (((1,), (1,)), ((), ())), preferred_element_type=jnp.float32
-        )
+        return jnp.dot(k_buf[slot], q_turned[ring], preferred_element_type=jnp.float32)
 
     def visit(units, fresh=False, finish=None):
         scores = [score(units[0][0], slot) for slot in units[0][1]]
@@ -304,6 +302,8 @@
         v_own[step].wait_recv()
     for mate in near:
         q_moves[mate].wait_recv()
+    turn_queries(0)
+    turn_queries(1)
     visit([(0, (0, 1, 2, 3)), (1, (0, 1, 2, 3))], fresh=True)
 
     for move in v_leg[1]:
@@ -323,6 +323,7 @@
     k_edge.start()
     for mate in distant[:2]:
         q_moves[mate].wait_recv()
+    turn_queries(2)
     visit([(2, (0, 1, 2)), (2, (3, 4, 5))], fresh=True)
 
     v_other["x"].wait_recv()
@@ -333,6 +334,7 @@
     visit([(ring, (6, 7, 8)) for ring in range(3)])
     for mate in distant[2:]:
         q_moves[mate].wait_recv()
+    turn_queries(3)
     visit([(3, (0, 1, 2)), (3, (3, 4, 5)), (3, (6, 7, 8))], fresh=True)
 
     for move in (k_other["z"], v_other["z"], k_edge, v_edge):
@@ -396,6 +398,7 @@
             pltpu.VMEM(spans[0].shape, jnp.int32),
             pltpu.VMEM(spans[1].shape, jnp.int32),
             pltpu.VMEM((KV_HEADS, rows, part), jnp.bfloat16),
+            pltpu.VMEM((4, HEAD_DIM, 256), jnp.bfloat16),
             pltpu.VMEM((SLOTS, tokens, HEAD_DIM), jnp.bfloat16),
             pltpu.VMEM((SLOTS, HEAD_DIM, tokens), jnp.bfloat16),
             pltpu.VMEM((tokens, HEAD_DIM), jnp.bfloat16),

time: 35.2 us -> 35.1 us (level)
  no operation moved by 1% of the time
where the time goes in v6:
time: 35.1 us; the launch traced here: 35 us
  Pallas kernels  34.3 us (98%)
  local copies, waits for them, and re-layouts  0.71 us (2%)
    pallas_call x1, Pallas kernels, shards(): pl.pallas_call(functools.partial(kernel, groups), out_shape=pltpu.VMEM((r...  34.3 us
    unnamed x1, local copies, waits for them, and re-layouts  0.71 us

profile of v6, /device:TPU:135, one launch (start us, length us, event | category | flops | bytes accessed | tf_op | source)
XLA Modules:
  0.0 35.0 jit_solution(6031341693683596145)
XLA Ops:
  0.0 34.3 %shard_map.55 = bf16[16,8192]{1,0:T(8,128)(2,1)S(1)} custom-call(bf16[16,8192]{1,0:T(8,128)(2,1)} %q_hbm.1, bf16[256,128]{1,0:T(8,128)(2,1)} %k_hbm.1, bf16[256,128]{1,0:T(8,128)(2,1)} %v_hbm.1, s32[1,128]{1,0:T(1,128)} %bitcast.2, s32[1,128]{1,0:T(1,128)} %bitcast.3), custom_call_target="tpu_custom_call" | custom-call | flops 1476395008 | bytes 1048576 | tf_op jit(solution)/shard_map/pallas_call | solution.py:392
  34.3 0.7 %copy.7 = bf16[16,8192]{1,0:T(8,128)(2,1)} copy(bf16[16,8192]{1,0:T(8,128)(2,1)S(1)} %shard_map.55) | data formatting | bytes 524288

commit v7 on v6

--- a/solution.py
+++ b/solution.py
@@ -60,12 +60,9 @@
         there = (4 * parity + chip + 8 + distance) % 8
         return {"tm": 2 * pair + there // 4, "head": 2 * (there % 4) + core}
 
-    def flip(value):
-        return value + 1 - 2 * (value % 2)
-
     def chunk_of(ring):
-        start = chip if ring < 2 else (chip + 2) % 4
-        return start if ring % 2 == 0 else flip(start)
+        start = (chip + 2 * (ring // 2)) % 4
+        return start + (ring % 2) * (1 - 2 * (start % 2))
 
     def columns(head):
         return pl.ds(pl.multiple_of(head * width, width), width)
@@ -247,7 +244,7 @@
         ones = jnp.ones((16, tokens), jnp.bfloat16)
         for at, (ring, slots) in enumerate(units):
             following = units[at + 1] if at + 1 < len(units) else (ring, ())
-            renew = fresh and all(ring != earlier for earlier, _ in units[:at])
+            renew = fresh and at == 0
             begin, end = first[ring], last[ring]
             inside, best = [], []
             for slot, part in zip(slots, scores):
@@ -272,12 +269,19 @@
                 gained = gained + jnp.dot(left, weights, preferred_element_type=jnp.float32)
             for slot in following[1][len(slots):]:
                 ahead.append(score(following[0], slot))
-            if finish is None:
+            if finish is not None:
+                finish(ring, gained)
+            else:
                 peak[ring] = top
                 total[ring] = gained
-            else:
-                finish(ring, gained)
             scores = ahead
+
+    def over_rings(count, slots, fresh=False):
+        def body(ring, carry):
+            visit([(ring, slots)], fresh)
+            return carry
+
+        lax.fori_loop(0, count, body, 0)
 
     for move, onward in zip(k_leg[0], k_leg[1]):
         move.wait_recv()
@@ -304,7 +308,7 @@
         q_moves[mate].wait_recv()
     turn_queries(0)
     turn_queries(1)
-    visit([(0, (0, 1, 2, 3)), (1, (0, 1, 2, 3))], fresh=True)
+    over_rings(2, (0, 1, 2, 3), fresh=True)
 
     for move in v_leg[1]:
         move.wait_recv()
@@ -314,7 +318,7 @@
         q_moves[mate].start()
     k_own["z"].wait_recv()
     v_own["z"].wait_recv()
-    visit([(0, (4, 5)), (1, (4, 5))])
+    over_rings(2, (4, 5))
 
     k_other["x"].wait_recv()
     k_other["z"].start()
@@ -331,7 +335,7 @@
     v_other[1].wait_recv()
     v_other[-1].wait_recv()
     v_edge.start()
-    visit([(ring, (6, 7, 8)) for ring in range(3)])
+    over_rings(3, (6, 7, 8))
     for mate in distant[2:]:
         q_moves[mate].wait_recv()
     turn_queries(3)
@@ -350,23 +354,32 @@
             {"tm": t, "head": target},
         )
 
-    o_moves = {mate: o_copy(*mate) for mate in mates}
     def send(ring, done):
         mean = done[:HEAD_DIM] / done[HEAD_DIM:HEAD_DIM + 1]
         turned = mean.T.astype(jnp.bfloat16)
         for b in range(2):
+            target = 2 * chunk_of(ring) + b
             for g in range(GROUP):
                 begin = (b * GROUP + g) * rows
-                ready[2 * chunk_of(ring) + b, :, g * HEAD_DIM:(g + 1) * HEAD_DIM] = turned[
-                    begin:begin + rows
-                ]
-        for mate in mates:
-            if mate[0] == ring:
-                o_moves[mate].start()
-        if ring == 0:
+                ready[target, :, g * HEAD_DIM:(g + 1) * HEAD_DIM] = turned[begin:begin + rows]
+
+    def last_stage(i, carry):
+        ring = 3 - i
+        visit([(ring, (9, 10))], finish=send)
+        o_copy(ring, 1).start()
+
+        @pl.when(ring > 0)
+        def _():
+            o_copy(ring, 0).start()
+
+        @pl.when(ring == 0)
+        def _():
             own_out.start()
 
-    visit([(ring, (9, 10)) for ring in (3, 2, 1, 0)], finish=send)
+        return carry
+
+    lax.fori_loop(0, 4, last_stage, 0)
+    o_moves = {mate: o_copy(*mate) for mate in mates}
 
     for moves in (k_own, v_own, k_other, v_other):
         for move in moves.values():

time: 35.1 us -> 35.3 us (level); the launches traced: 35 us -> 34.8 us
  no operation moved by 1% of the time
where the time goes in v7:
time: 35.3 us; the launch traced here: 34.8 us
  Pallas kernels  34.1 us (97%)
  local copies, waits for them, and re-layouts  0.71 us (2%)
    pallas_call x1, Pallas kernels, shards(): pl.pallas_call(functools.partial(kernel, groups), out_shape=pltpu.VMEM((r...  34.1 us

profile of v7, /device:TPU:135, one launch (start us, length us, event | category | flops | bytes accessed | tf_op | source)
XLA Modules:
  0.0 34.8 jit_solution(15898808646626027817)
XLA Ops:
  0.0 34.1 %shard_map.55 = bf16[16,8192]{1,0:T(8,128)(2,1)S(1)} custom-call(bf16[16,8192]{1,0:T(8,128)(2,1)} %q_hbm.1, bf16[256,128]{1,0:T(8,128)(2,1)} %k_hbm.1, bf16[256,128]{1,0:T(8,128)(2,1)} %v_hbm.1, s32[1,128]{1,0:T(1,128)} %bitcast.2, s32[1,128]{1,0:T(1,128)} %bitcast.3), custom_call_target="tpu_custom_call" | custom-call | flops 1476395008 | bytes 1048576 | tf_op jit(solution)/shard_map/pallas_call | solution.py:405
  34.1 0.7 %copy.7 = bf16[16,8192]{1,0:T(8,128)(2,1)} copy(bf16[16,8192]{1,0:T(8,128)(2,1)S(1)} %shard_map.55) | data formatting | bytes 524288

commit v8 on v6

--- a/solution.py
+++ b/solution.py
@@ -242,12 +242,12 @@
     def score(ring, slot):
         return jnp.dot(k_buf[slot], q_turned[ring], preferred_element_type=jnp.float32)
 
-    def visit(units, fresh=False, finish=None):
+    def visit(units, fresh=(), finish=None):
         scores = [score(units[0][0], slot) for slot in units[0][1]]
         ones = jnp.ones((16, tokens), jnp.bfloat16)
         for at, (ring, slots) in enumerate(units):
             following = units[at + 1] if at + 1 < len(units) else (ring, ())
-            renew = fresh and all(ring != earlier for earlier, _ in units[:at])
+            renew = ring in fresh and all(ring != earlier for earlier, _ in units[:at])
             begin, end = first[ring], last[ring]
             inside, best = [], []
             for slot, part in zip(slots, scores):
@@ -304,7 +304,7 @@
         q_moves[mate].wait_recv()
     turn_queries(0)
     turn_queries(1)
-    visit([(0, (0, 1, 2, 3)), (1, (0, 1, 2, 3))], fresh=True)
+    visit([(0, (0, 1, 2, 3)), (1, (0, 1, 2, 3))], fresh=(0, 1))
 
     for move in v_leg[1]:
         move.wait_recv()
@@ -314,8 +314,6 @@
         q_moves[mate].start()
     k_own["z"].wait_recv()
     v_own["z"].wait_recv()
-    visit([(0, (4, 5)), (1, (4, 5))])
-
     k_other["x"].wait_recv()
     k_other["z"].start()
     k_other[1].wait_recv()
@@ -324,18 +322,18 @@
     for mate in distant[:2]:
         q_moves[mate].wait_recv()
     turn_queries(2)
-    visit([(2, (0, 1, 2)), (2, (3, 4, 5))], fresh=True)
+    visit([(2, (0, 1, 2)), (0, (4, 5)), (2, (3, 4, 5)), (1, (4, 5))], fresh=(2,))
 
     v_other["x"].wait_recv()
     v_other["z"].start()
     v_other[1].wait_recv()
     v_other[-1].wait_recv()
     v_edge.start()
-    visit([(ring, (6, 7, 8)) for ring in range(3)])
     for mate in distant[2:]:
         q_moves[mate].wait_recv()
     turn_queries(3)
-    visit([(3, (0, 1, 2)), (3, (3, 4, 5)), (3, (6, 7, 8))], fresh=True)
+    units = [(3, (0, 1, 2)), (0, (6, 7, 8)), (3, (3, 4, 5)), (1, (6, 7, 8)), (3, (6, 7, 8))]
+    visit(units + [(2, (6, 7, 8))], fresh=(3,))
 
     for move in (k_other["z"], v_other["z"], k_edge, v_edge):
         move.wait_recv()
@@ -352,8 +350,8 @@
 
     o_moves = {mate: o_copy(*mate) for mate in mates}
     def send(ring, done):
-        mean = done[:HEAD_DIM] / done[HEAD_DIM:HEAD_DIM + 1]
-        turned = mean.T.astype(jnp.bfloat16)
+        mean = done[:HEAD_DIM] * (1.0 / done[HEAD_DIM:HEAD_DIM + 1])
+        turned = mean.astype(jnp.bfloat16).T
         for b in range(2):
             for g in range(GROUP):
                 begin = (b * GROUP + g) * rows

time: 35.1 us -> 35.5 us (1.011)
  the two profiles are of different devices: /device:TPU:135 before, /device:TPU:191 now
where the time goes in v8:
time: 35.5 us; the launch traced here: 35.4 us
  Pallas kernels  34.7 us (98%)
  local copies, waits for them, and re-layouts  0.71 us (2%)
    pallas_call x1, Pallas kernels, shards(): pl.pallas_call(functools.partial(kernel, groups), out_shape=pltpu.VMEM((r...  34.7 us

profile of v8, /device:TPU:191, one launch (start us, length us, event | category | flops | bytes accessed | tf_op | source)
XLA Modules:
  0.0 35.4 jit_solution(11120795227546392406)
XLA Ops:
  0.0 34.7 %shard_map.55 = bf16[16,8192]{1,0:T(8,128)(2,1)S(1)} custom-call(bf16[16,8192]{1,0:T(8,128)(2,1)} %q_hbm.1, bf16[256,128]{1,0:T(8,128)(2,1)} %k_hbm.1, bf16[256,128]{1,0:T(8,128)(2,1)} %v_hbm.1, s32[1,128]{1,0:T(1,128)} %bitcast.2, s32[1,128]{1,0:T(1,128)} %bitcast.3), custom_call_target="tpu_custom_call" | custom-call | flops 1476395008 | bytes 1048576 | tf_op jit(solution)/shard_map/pallas_call | solution.py:390
  34.7 0.7 %copy.7 = bf16[16,8192]{1,0:T(8,128)(2,1)} copy(bf16[16,8192]{1,0:T(8,128)(2,1)S(1)} %shard_map.55) | data formatting | bytes 524288

commit v9 on v6

--- a/solution.py
+++ b/solution.py
@@ -200,28 +200,6 @@
         v_own[step].start()
     for mate in ((1, 0), (1, 1)):
         q_moves[mate].start()
-
-    unused = [(base[d], jnp.logical_not(has(d))) for base in (OWN, PAIR) for d in (1, -1)]
-    unused += [(base["z"], jnp.where(low, at_start, at_end)) for base in (OWN, PAIR)]
-    unused.append((EDGE, jnp.logical_not(jnp.where(parity == 0, has(-3), has(3)))))
-    for slot, empty in unused:
-        @pl.when(empty)
-        def _(slot=slot):
-            k_buf[slot] = jnp.zeros(k_buf.shape[1:], k_buf.dtype)
-            v_buf[slot] = jnp.zeros(v_buf.shape[1:], v_buf.dtype)
-
-    for load in span_loads:
-        load.wait()
-    lane = lax.broadcasted_iota(jnp.int32, (128, 256), 1)
-    row = lax.broadcasted_iota(jnp.int32, (128, 256), 0)
-    for ring in range(4):
-        wanted = chunk_of(ring) * 32 + (lane // 128) * 16 + lane % 16
-        chosen = jnp.where(row == wanted, 1.0, 0.0).astype(jnp.bfloat16)
-        for ref, held in ((first_ref, first), (last_ref, last)):
-            offset_row = (ref[...] - t).astype(jnp.float32)
-            offset_row = jnp.broadcast_to(offset_row, (16, 128)).astype(jnp.bfloat16)
-            placed = jnp.dot(offset_row, chosen, preferred_element_type=jnp.float32)
-            held[ring] = placed[0:1]
 
     def offset(slot):
         places = {"x": jnp.where(low, 2, -2), "z": jnp.where(low, -2, 2)}
@@ -295,6 +273,34 @@
         k_other[step].start()
     v_own["x"].wait_recv()
     v_own["z"].start()
+    for move in v_leg[1]:
+        move.wait_recv()
+    for step in ("x", 1, -1):
+        v_other[step].start()
+    for mate in distant[2:]:
+        q_moves[mate].start()
+    unused = [(base[d], jnp.logical_not(has(d))) for base in (OWN, PAIR) for d in (1, -1)]
+    unused += [(base["z"], jnp.where(low, at_start, at_end)) for base in (OWN, PAIR)]
+    unused.append((EDGE, jnp.logical_not(jnp.where(parity == 0, has(-3), has(3)))))
+    for slot, empty in unused:
+        @pl.when(empty)
+        def _(slot=slot):
+            k_buf[slot] = jnp.zeros(k_buf.shape[1:], k_buf.dtype)
+            v_buf[slot] = jnp.zeros(v_buf.shape[1:], v_buf.dtype)
+
+    for load in span_loads:
+        load.wait()
+    lane = lax.broadcasted_iota(jnp.int32, (128, 256), 1)
+    row = lax.broadcasted_iota(jnp.int32, (128, 256), 0)
+    for ring in range(4):
+        wanted = chunk_of(ring) * 32 + (lane // 128) * 16 + lane % 16
+        chosen = jnp.where(row == wanted, 1.0, 0.0).astype(jnp.bfloat16)
+        for ref, held in ((first_ref, first), (last_ref, last)):
+            offset_row = (ref[...] - t).astype(jnp.float32)
+            offset_row = jnp.broadcast_to(offset_row, (16, 128)).astype(jnp.bfloat16)
+            placed = jnp.dot(offset_row, chosen, preferred_element_type=jnp.float32)
+            held[ring] = placed[0:1]
+
     k_load.wait()
     q_load.wait()
     for step in (1, -1):
@@ -306,12 +312,6 @@
     turn_queries(1)
     visit([(0, (0, 1, 2, 3)), (1, (0, 1, 2, 3))], fresh=True)
 
-    for move in v_leg[1]:
-        move.wait_recv()
-    for step in ("x", 1, -1):
-        v_other[step].start()
-    for mate in distant[2:]:
-        q_moves[mate].start()
     k_own["z"].wait_recv()
     v_own["z"].wait_recv()
     visit([(0, (4, 5)), (1, (4, 5))])

time: 35.1 us -> 35.1 us (level)
  no operation moved by 1% of the time
where the time goes in v9:
time: 35.1 us; the launch traced here: 35 us
  Pallas kernels  34.3 us (98%)
  local copies, waits for them, and re-layouts  0.71 us (2%)
    pallas_call x1, Pallas kernels, shards(): pl.pallas_call(functools.partial(kernel, groups), out_shape=pltpu.VMEM((r...  34.3 us
    unnamed x1, local copies, waits for them, and re-layouts  0.71 us

profile of v9, /device:TPU:135, one launch (start us, length us, event | category | flops | bytes accessed | tf_op | source)
XLA Modules:
  0.0 35.0 jit_solution(7586466758037861238)
XLA Ops:
  0.0 34.3 %shard_map.55 = bf16[16,8192]{1,0:T(8,128)(2,1)S(1)} custom-call(bf16[16,8192]{1,0:T(8,128)(2,1)} %q_hbm.1, bf16[256,128]{1,0:T(8,128)(2,1)} %k_hbm.1, bf16[256,128]{1,0:T(8,128)(2,1)} %v_hbm.1, s32[1,128]{1,0:T(1,128)} %bitcast.2, s32[1,128]{1,0:T(1,128)} %bitcast.3), custom_call_target="tpu_custom_call" | custom-call | flops 1476395008 | bytes 1048576 | tf_op jit(solution)/shard_map/pallas_call | solution.py:392
  34.3 0.7 %copy.7 = bf16[16,8192]{1,0:T(8,128)(2,1)} copy(bf16[16,8192]{1,0:T(8,128)(2,1)S(1)} %shard_map.55) | data formatting | bytes 524288

commit v10 on v9

--- a/solution.py
+++ b/solution.py
@@ -64,7 +64,7 @@
         return value + 1 - 2 * (value % 2)
 
     def chunk_of(ring):
-        start = chip if ring < 2 else (chip + 2) % 4
+        start = chip if ring < 2 else 3 - chip
         return start if ring % 2 == 0 else flip(start)
 
     def columns(head):
@@ -192,8 +192,6 @@
     q_moves[0, 1].start()
     v_load.wait()
     v_buf[OWN[0]] = v_rows[...].T
-    for move in k_leg[0]:
-        move.wait_send()
     for move in v_leg[0]:
         move.start()
     for step in first_steps:
@@ -366,12 +364,12 @@
         if ring == 0:
             own_out.start()
 
-    visit([(ring, (9, 10)) for ring in (3, 2, 1, 0)], finish=send)
+    visit([(ring, (9, 10)) for ring in (2, 3, 1, 0)], finish=send)
 
     for moves in (k_own, v_own, k_other, v_other):
         for move in moves.values():
             move.wait_send()
-    for move in (k_edge, v_edge, *k_leg[1], *v_leg[0], *v_leg[1]):
+    for move in (k_edge, v_edge, *k_leg[0], *k_leg[1], *v_leg[0], *v_leg[1]):
         move.wait_send()
     for move in q_moves.values():
         move.wait_send()

time: 35.1 us -> 35.3 us (level)
  no operation moved by 1% of the time
where the time goes in v10:
time: 35.3 us; the launch traced here: 35.1 us
  Pallas kernels  34.4 us (97%)
  local copies, waits for them, and re-layouts  0.71 us (2%)
    pallas_call x1, Pallas kernels, shards(): pl.pallas_call(functools.partial(kernel, groups), out_shape=pltpu.VMEM((r...  34.4 us

profile of v10, /device:TPU:135, one launch (start us, length us, event | category | flops | bytes accessed | tf_op | source)
XLA Modules:
  0.0 35.1 jit_solution(13111755531910282087)
XLA Ops:
  0.0 34.4 %shard_map.55 = bf16[16,8192]{1,0:T(8,128)(2,1)S(1)} custom-call(bf16[16,8192]{1,0:T(8,128)(2,1)} %q_hbm.1, bf16[256,128]{1,0:T(8,128)(2,1)} %k_hbm.1, bf16[256,128]{1,0:T(8,128)(2,1)} %v_hbm.1, s32[1,128]{1,0:T(1,128)} %bitcast.2, s32[1,128]{1,0:T(1,128)} %bitcast.3), custom_call_target="tpu_custom_call" | custom-call | flops 1476395008 | bytes 1048576 | tf_op jit(solution)/shard_map/pallas_call | solution.py:390
  34.4 0.7 %copy.7 = bf16[16,8192]{1,0:T(8,128)(2,1)} copy(bf16[16,8192]{1,0:T(8,128)(2,1)S(1)} %shard_map.55) | data formatting | bytes 524288

commit v11 on v9

--- a/solution.py
+++ b/solution.py
@@ -39,7 +39,7 @@
 
 def kernel(
     groups, q_hbm, k_hbm, v_hbm, first_hbm, last_hbm, out_ref, first_ref, last_ref,
-    q_buf, q_turned, k_buf, v_buf, k_relay, v_relay, v_rows, total, peak, first, last, ready,
+    q_buf, q_turned, k_buf, v_buf, v_rows, total, peak, first, last, ready,
     local_sem, q_send, q_recv, k_send, k_recv, v_send, v_recv, o_send, o_recv,
 ):
     t = lax.axis_index("tm")
@@ -56,10 +56,6 @@
     def at_pair(distance):
         return {"tm": (t + groups + 2 * distance) % groups, "head": h}
 
-    def along_y(distance):
-        there = (4 * parity + chip + 8 + distance) % 8
-        return {"tm": 2 * pair + there // 4, "head": 2 * (there % 4) + core}
-
     def flip(value):
         return value + 1 - 2 * (value % 2)
 
@@ -110,7 +106,7 @@
         return (pair >= -distance) if distance < 0 else (pair < pairs - distance)
 
     barrier = pltpu.get_barrier_semaphore()
-    everywhere = [along_y(2), along_y(-2), opposite_x]
+    everywhere = [{"tm": t + side, "head": h}, opposite_x]
     everywhere += [{"tm": t, "head": head_of(*mate)} for mate in mates]
     for partner in everywhere:
         pl.semaphore_signal(barrier, inc=1, device_id=partner, device_id_type=MESH)
@@ -159,22 +155,9 @@
             jnp.where(up, to_last | (x == 3), to_next | (x == 0)),
         )
 
-    def legs(copy, buf, source, passing):
-        half = passing.shape[0] // 2
-        parts = ((pl.ds(0, half), 2, 0, 11), (pl.ds(half, half), -2, 10, 12))
-        return [
-            [
-                copy(source.at[part], passing.at[part], role, along_y(way))
-                for part, way, role, _ in parts
-            ],
-            [
-                copy(passing.at[part], buf.at[PAIR[0], part], role, along_y(way))
-                for part, way, _, role in parts
-            ],
-        ]
-
-    k_leg = legs(k_copy, k_buf, k_hbm, k_relay)
-    v_leg = legs(v_copy, v_buf, v_buf.at[OWN[0]], v_relay)
+    partner = {"tm": t + side, "head": h}
+    k_pair = k_copy(k_hbm, k_buf.at[PAIR[0]], 0, partner)
+    v_pair = v_copy(v_buf.at[OWN[0]], v_buf.at[PAIR[0]], 0, partner)
     k_own = spread(k_copy, k_buf, OWN, 1, k_hbm)
     v_own = spread(v_copy, v_buf, OWN, 1, v_buf.at[OWN[0]])
     k_other = spread(k_copy, k_buf, PAIR, 5, k_buf.at[PAIR[0]])
@@ -185,17 +168,13 @@
     pl.semaphore_wait(barrier, answers)
 
     first_steps = (1, -1, "x")
-    for move in k_leg[0]:
-        move.start()
+    k_pair.start()
     for step in first_steps:
         k_own[step].start()
     q_moves[0, 1].start()
     v_load.wait()
     v_buf[OWN[0]] = v_rows[...].T
-    for move in k_leg[0]:
-        move.wait_send()
-    for move in v_leg[0]:
-        move.start()
+    v_pair.start()
     for step in first_steps:
         v_own[step].start()
     for mate in ((1, 0), (1, 1)):
@@ -257,24 +236,16 @@
                 finish(ring, gained)
             scores = ahead
 
-    for move, onward in zip(k_leg[0], k_leg[1]):
-        move.wait_recv()
-        onward.start()
     k_own["x"].wait_recv()
     k_own["z"].start()
-    for move, onward in zip(v_leg[0], v_leg[1]):
-        move.wait_recv()
-        onward.start()
+    k_pair.wait_recv()
+    for step in ("x", 1, -1):
+        k_other[step].start()
     for mate in distant[:2]:
         q_moves[mate].start()
-    for move in k_leg[1]:
-        move.wait_recv()
-    for step in ("x", 1, -1):
-        k_other[step].start()
     v_own["x"].wait_recv()
     v_own["z"].start()
-    for move in v_leg[1]:
-        move.wait_recv()
+    v_pair.wait_recv()
     for step in ("x", 1, -1):
         v_other[step].start()
     for mate in distant[2:]:
@@ -371,7 +342,7 @@
     for moves in (k_own, v_own, k_other, v_other):
         for move in moves.values():
             move.wait_send()
-    for move in (k_edge, v_edge, *k_leg[1], *v_leg[0], *v_leg[1]):
+    for move in (k_edge, v_edge, k_pair, v_pair):
         move.wait_send()
     for move in q_moves.values():
         move.wait_send()
@@ -402,8 +373,6 @@
             pltpu.VMEM((SLOTS, tokens, HEAD_DIM), jnp.bfloat16),
             pltpu.VMEM((SLOTS, HEAD_DIM, tokens), jnp.bfloat16),
             pltpu.VMEM((tokens, HEAD_DIM), jnp.bfloat16),
-            pltpu.VMEM((HEAD_DIM, tokens), jnp.bfloat16),
-            pltpu.VMEM((tokens, HEAD_DIM), jnp.bfloat16),
             pltpu.VMEM((4, HEAD_DIM + 16, 256), jnp.float32),
             pltpu.VMEM((4, 1, 256), jnp.float32),
             pltpu.VMEM((4, 1, 256), jnp.float32),
@@ -412,10 +381,10 @@
             dma((6,)),
             dma((8,)),
             dma((8,)),
-            dma((13,)),
-            dma((13,)),
-            dma((13,)),
-            dma((13,)),
+            dma((10,)),
+            dma((10,)),
+            dma((10,)),
+            dma((10,)),
             dma((8,)),
             dma((8,)),
         ],

time: 35.1 us -> 35.3 us (level)
  no operation moved by 1% of the time
where the time goes in v11:
time: 35.3 us; the launch traced here: 35.1 us
  Pallas kernels  34.4 us (97%)
  local copies, waits for them, and re-layouts  0.71 us (2%)
    pallas_call x1, Pallas kernels, shards(): pl.pallas_call(functools.partial(kernel, groups), out_shape=pltpu.VMEM((r...  34.4 us

profile of v11, /device:TPU:135, one launch (start us, length us, event | category | flops | bytes accessed | tf_op | source)
XLA Modules:
  0.0 35.1 jit_solution(9668657782836488538)
XLA Ops:
  0.0 34.4 %shard_map.55 = bf16[16,8192]{1,0:T(8,128)(2,1)S(1)} custom-call(bf16[16,8192]{1,0:T(8,128)(2,1)} %q_hbm.1, bf16[256,128]{1,0:T(8,128)(2,1)} %k_hbm.1, bf16[256,128]{1,0:T(8,128)(2,1)} %v_hbm.1, s32[1,128]{1,0:T(1,128)} %bitcast.2, s32[1,128]{1,0:T(1,128)} %bitcast.3), custom_call_target="tpu_custom_call" | custom-call | flops 1476395008 | bytes 1048576 | tf_op jit(solution)/shard_map/pallas_call | solution.py:363
  34.4 0.7 %copy.7 = bf16[16,8192]{1,0:T(8,128)(2,1)} copy(bf16[16,8192]{1,0:T(8,128)(2,1)S(1)} %shard_map.55) | data formatting | bytes 524288

commit v12 on v11

--- a/solution.py
+++ b/solution.py
@@ -112,9 +112,13 @@
         pl.semaphore_signal(barrier, inc=1, device_id=partner, device_id_type=MESH)
     answers = len(everywhere)
     corner = jnp.where(parity == 0, pair == 0, pair == pairs - 1)
-    cornered = jnp.where(parity == 0, pair == 3, pair == pairs - 4)
+    low = x < 2
+    to_next, to_last = jnp.logical_not(at_end), jnp.logical_not(at_start)
+    beyond = jnp.where(low, to_last, to_next), at_pair(jnp.where(low, -2, 2))
+    ahead = jnp.where(parity == 0, has(3), has(-3)), at_pair(3 * side)
+    behind = jnp.where(parity == 0, has(-3), has(3)), at_pair(-3 * side)
     others = [(has(distance), at_pair(distance)) for distance in (1, -1, 4, -4)]
-    others += [(corner, at_pair(3 * side)), (cornered, at_pair(-3 * side))]
+    others += [beyond, ahead, behind]
     for present, partner in others:
         answers = answers + jnp.where(present, 1, 0)
 
@@ -125,8 +129,6 @@
     for load in (v_load, k_load, *span_loads, q_load):
         load.start()
 
-    low = x < 2
-    to_next, to_last = jnp.logical_not(at_end), jnp.logical_not(at_start)
 
     def spread(copy, buf, base, role, source):
         moves = {
@@ -162,7 +164,14 @@
     v_own = spread(v_copy, v_buf, OWN, 1, v_buf.at[OWN[0]])
     k_other = spread(k_copy, k_buf, PAIR, 5, k_buf.at[PAIR[0]])
     v_other = spread(v_copy, v_buf, PAIR, 5, v_buf.at[PAIR[0]])
-    k_edge, v_edge = edge(k_copy, k_buf), edge(v_copy, v_buf)
+    k_edge = edge(k_copy, k_buf)
+    v_other["z"] = Move(
+        [(beyond[0], v_copy(v_buf.at[PAIR[0]], v_buf.at[PAIR["z"]], 8, beyond[1]))],
+        v_other["z"].arrives,
+    )
+    v_edge = Move(
+        [(ahead[0], v_copy(v_buf.at[PAIR[0]], v_buf.at[EDGE], 9, ahead[1]))], behind[0]
+    )
     q_moves = {mate: q_copy(*mate) for mate in mates}
 
     pl.semaphore_wait(barrier, answers)
@@ -246,8 +255,9 @@
     v_own["x"].wait_recv()
     v_own["z"].start()
     v_pair.wait_recv()
-    for step in ("x", 1, -1):
+    for step in ("x", "z", 1, -1):
         v_other[step].start()
+    v_edge.start()
     for mate in distant[2:]:
         q_moves[mate].start()
     unused = [(base[d], jnp.logical_not(has(d))) for base in (OWN, PAIR) for d in (1, -1)]
@@ -297,11 +307,8 @@
     turn_queries(2)
     visit([(2, (0, 1, 2)), (2, (3, 4, 5))], fresh=True)
 
-    v_other["x"].wait_recv()
-    v_other["z"].start()
-    v_other[1].wait_recv()
-    v_other[-1].wait_recv()
-    v_edge.start()
+    for step in ("x", 1, -1):
+        v_other[step].wait_recv()
     visit([(ring, (6, 7, 8)) for ring in range(3)])
     for mate in distant[2:]:
         q_moves[mate].wait_recv()

time: 35.3 us -> 35.3 us (level)
  the two profiles are of different devices: /device:TPU:135 before, /device:TPU:259 now
where the time goes in v12:
time: 35.3 us; the launch traced here: 35.1 us
  Pallas kernels  34.4 us (97%)
  local copies, waits for them, and re-layouts  0.71 us (2%)
    pallas_call x1, Pallas kernels, shards(): pl.pallas_call(functools.partial(kernel, groups), out_shape=pltpu.VMEM((r...  34.4 us

profile of v12, /device:TPU:259, one launch (start us, length us, event | category | flops | bytes accessed | tf_op | source)
XLA Modules:
  0.0 35.1 jit_solution(1734976976235903456)
XLA Ops:
  0.0 34.4 %shard_map.55 = bf16[16,8192]{1,0:T(8,128)(2,1)S(1)} custom-call(bf16[16,8192]{1,0:T(8,128)(2,1)} %q_hbm.1, bf16[256,128]{1,0:T(8,128)(2,1)} %k_hbm.1, bf16[256,128]{1,0:T(8,128)(2,1)} %v_hbm.1, s32[1,128]{1,0:T(1,128)} %bitcast.2, s32[1,128]{1,0:T(1,128)} %bitcast.3), custom_call_target="tpu_custom_call" | custom-call | flops 1476395008 | bytes 1048576 | tf_op jit(solution)/shard_map/pallas_call | solution.py:370
  34.4 0.7 %copy.7 = bf16[16,8192]{1,0:T(8,128)(2,1)} copy(bf16[16,8192]{1,0:T(8,128)(2,1)S(1)} %shard_map.55) | data formatting | bytes 524288

commit v13 on v12

--- a/solution.py
+++ b/solution.py
@@ -129,8 +129,7 @@
     for load in (v_load, k_load, *span_loads, q_load):
         load.start()
 
-
-    def spread(copy, buf, base, role, source):
+    def spread(copy, buf, base, role, source, relayed=True):
         moves = {
             e: Move(
                 [(has(e), copy(source, buf.at[base[-e]], role + i, at_pair(e)))],
@@ -139,12 +138,12 @@
             for i, e in enumerate((1, -1))
         }
         moves["x"] = copy(source, buf.at[base["x"]], role + 2, opposite_x)
-        along = copy(
-            buf.at[base["x"]], buf.at[base["z"]], role + 3, at_pair(jnp.where(low, 4, -4))
-        )
-        moves["z"] = Move(
-            [(jnp.where(low, to_next, to_last), along)], jnp.where(low, to_last, to_next)
-        )
+        if relayed:
+            leaves, target, held = jnp.where(low, to_next, to_last), jnp.where(low, 4, -4), "x"
+        else:
+            leaves, target, held = beyond[0], jnp.where(low, -2, 2), 0
+        along = copy(buf.at[base[held]], buf.at[base["z"]], role + 3, at_pair(target))
+        moves["z"] = Move([(leaves, along)], beyond[0])
         return moves
 
     def edge(copy, buf):
@@ -163,12 +162,8 @@
     k_own = spread(k_copy, k_buf, OWN, 1, k_hbm)
     v_own = spread(v_copy, v_buf, OWN, 1, v_buf.at[OWN[0]])
     k_other = spread(k_copy, k_buf, PAIR, 5, k_buf.at[PAIR[0]])
-    v_other = spread(v_copy, v_buf, PAIR, 5, v_buf.at[PAIR[0]])
+    v_other = spread(v_copy, v_buf, PAIR, 5, v_buf.at[PAIR[0]], relayed=False)
     k_edge = edge(k_copy, k_buf)
-    v_other["z"] = Move(
-        [(beyond[0], v_copy(v_buf.at[PAIR[0]], v_buf.at[PAIR["z"]], 8, beyond[1]))],
-        v_other["z"].arrives,
-    )
     v_edge = Move(
         [(ahead[0], v_copy(v_buf.at[PAIR[0]], v_buf.at[EDGE], 9, ahead[1]))], behind[0]
     )
@@ -307,13 +302,14 @@
     turn_queries(2)
     visit([(2, (0, 1, 2)), (2, (3, 4, 5))], fresh=True)
 
-    for step in ("x", 1, -1):
-        v_other[step].wait_recv()
-    visit([(ring, (6, 7, 8)) for ring in range(3)])
     for mate in distant[2:]:
         q_moves[mate].wait_recv()
     turn_queries(3)
-    visit([(3, (0, 1, 2)), (3, (3, 4, 5)), (3, (6, 7, 8))], fresh=True)
+    visit([(3, (0, 1, 2)), (3, (3, 4, 5))], fresh=True)
+
+    for step in ("x", 1, -1):
+        v_other[step].wait_recv()
+    visit([(ring, (6, 7, 8)) for ring in range(4)])
 
     for move in (k_other["z"], v_other["z"], k_edge, v_edge):
         move.wait_recv()

time: 35.3 us -> 34.6 us (0.980)
  the two profiles are of different devices: /device:TPU:259 before, /device:TPU:1 now
where the time goes in v13:
time: 34.6 us; the launch traced here: 34.4 us
  Pallas kernels  33.7 us (97%)
  local copies, waits for them, and re-layouts  0.71 us (2%)
    pallas_call x1, Pallas kernels, shards(): pl.pallas_call(functools.partial(kernel, groups), out_shape=pltpu.VMEM((r...  33.7 us
    unnamed x1, local copies, waits for them, and re-layouts  0.71 us

profile of v13, /device:TPU:1, one launch (start us, length us, event | category | flops | bytes accessed | tf_op | source)
XLA Modules:
  0.0 34.4 jit_solution(15763024862551742400)
XLA Ops:
  0.0 33.7 %shard_map.55 = bf16[16,8192]{1,0:T(8,128)(2,1)S(1)} custom-call(bf16[16,8192]{1,0:T(8,128)(2,1)} %q_hbm.1, bf16[256,128]{1,0:T(8,128)(2,1)} %k_hbm.1, bf16[256,128]{1,0:T(8,128)(2,1)} %v_hbm.1, s32[1,128]{1,0:T(1,128)} %bitcast.2, s32[1,128]{1,0:T(1,128)} %bitcast.3), custom_call_target="tpu_custom_call" | custom-call | flops 1476395008 | bytes 1048576 | tf_op jit(solution)/shard_map/pallas_call | solution.py:366
  33.7 0.7 %copy.7 = bf16[16,8192]{1,0:T(8,128)(2,1)} copy(bf16[16,8192]{1,0:T(8,128)(2,1)S(1)} %shard_map.55) | data formatting | bytes 524288

commit v14 on v13

--- a/solution.py
+++ b/solution.py
@@ -60,7 +60,7 @@
         return value + 1 - 2 * (value % 2)
 
     def chunk_of(ring):
-        start = chip if ring < 2 else (chip + 2) % 4
+        start = chip if ring < 2 else 3 - chip
         return start if ring % 2 == 0 else flip(start)
 
     def columns(head):
@@ -325,8 +325,9 @@
         )
 
     o_moves = {mate: o_copy(*mate) for mate in mates}
+
     def send(ring, done):
-        mean = done[:HEAD_DIM] / done[HEAD_DIM:HEAD_DIM + 1]
+        mean = done[:HEAD_DIM] * (1.0 / done[HEAD_DIM:HEAD_DIM + 1])
         turned = mean.T.astype(jnp.bfloat16)
         for b in range(2):
             for g in range(GROUP):
@@ -340,7 +341,7 @@
         if ring == 0:
             own_out.start()
 
-    visit([(ring, (9, 10)) for ring in (3, 2, 1, 0)], finish=send)
+    visit([(ring, (9, 10)) for ring in (2, 3, 1, 0)], finish=send)
 
     for moves in (k_own, v_own, k_other, v_other):
         for move in moves.values():

time: 34.6 us -> 34.5 us (level)
  the two profiles are of different devices: /device:TPU:1 before, /device:TPU:129 now
where the time goes in v14:
time: 34.5 us; the launch traced here: 34.4 us
  Pallas kernels  33.7 us (98%)
  local copies, waits for them, and re-layouts  0.71 us (2%)
    pallas_call x1, Pallas kernels, shards(): pl.pallas_call(functools.partial(kernel, groups), out_shape=pltpu.VMEM((r...  33.7 us
    unnamed x1, local copies, waits for them, and re-layouts  0.71 us

profile of v14, /device:TPU:129, one launch (start us, length us, event | category | flops | bytes accessed | tf_op | source)
XLA Modules:
  0.0 34.4 jit_solution(14052766472713157014)
XLA Ops:
  0.0 33.7 %shard_map.55 = bf16[16,8192]{1,0:T(8,128)(2,1)S(1)} custom-call(bf16[16,8192]{1,0:T(8,128)(2,1)} %q_hbm.1, bf16[256,128]{1,0:T(8,128)(2,1)} %k_hbm.1, bf16[256,128]{1,0:T(8,128)(2,1)} %v_hbm.1, s32[1,128]{1,0:T(1,128)} %bitcast.2, s32[1,128]{1,0:T(1,128)} %bitcast.3), custom_call_target="tpu_custom_call" | custom-call | flops 1476395008 | bytes 1048576 | tf_op jit(solution)/shard_map/pallas_call | solution.py:367
  33.7 0.7 %copy.7 = bf16[16,8192]{1,0:T(8,128)(2,1)} copy(bf16[16,8192]{1,0:T(8,128)(2,1)S(1)} %shard_map.55) | data formatting | bytes 524288
